TPU v7x, 128 devices: a whole 4x4x4 slice. The times are simulated.
128 devices in a mesh: wide: 32 (over z, x_lo, y), narrow: 4 (over x_hi, core).
Axes of the slice: x: 4 (x_hi: 2, x_lo: 2; x = x_hi * 2 + x_lo), y: 4, z: 4, core: 2. Of those that a mesh axis runs over, the one named last changes fastest.
Arguments:
- features: bfloat16 [524288, 128], P(('wide', 'narrow')), may hold values from -6 to 6
- cotangent: bfloat16 [524288, 256], P(('wide', 'narrow')), may hold values from -6 to 6
- w_self: bfloat16 [128, 256], replicated, may hold values from -0.5 to 0.5
- w_neigh: bfloat16 [128, 256], replicated, may hold values from -0.5 to 0.5
- bias: float32 [256], replicated, may hold values from -4 to 4
- tile_weights: bfloat16 [65536, 128, 128], P(('wide', 'narrow')), may hold values from -0.125 to 0.125
- tile_src: int32 [65536], P(('wide', 'narrow')), may hold values from 0 to 47
- tile_dst: int32 [65536], P(('wide', 'narrow')), may hold values from 0 to 31
- tile_live: int32 [65536], P(('wide', 'narrow')), may hold values 0 or 1
- send_rows: int32 [4096, 32], P(('wide', 'narrow')), may hold values from 0 to 4095
- hub_rows: int32 [1024], P(('wide', 'narrow')), may hold values from 0 to 4095
Outputs:
- hidden: bfloat16 [524288, 256], P(('wide', 'narrow'))
- grad_features: float32 [524288, 128], P(('wide', 'narrow'))
- grad_self: float32 [128, 256], replicated
- grad_neigh: float32 [128, 256], replicated
- grad_bias: float32 [256], replicated
All inputs are finite; a program needn't handle non-finite values. No bound on the sum of `tile_live` on one device may be relied on, other than what follows from the above.
Results may differ from a plain program's by a relative error of at most 0.007.
Values may be sent and summed in bfloat16 or wider, within the bound.
A program may use at most 192 MiB of HBM per device.

v0:
```python
import jax
import jax.numpy as jnp
from jax import lax
from jax.sharding import PartitionSpec as P

TILE = 128


def gelu_tanh(value):
    return jax.nn.gelu(value, approximate=True)


def on_device(
    features,
    cotangent,
    w_self,
    w_neigh,
    bias,
    tile_weights,
    tile_src,
    tile_dst,
    tile_live,
    send_rows,
    hub_rows,
):
    nodes = features.shape[0]
    width = features.shape[1]
    peers = send_rows.shape[0]
    slots = send_rows.shape[1]
    owned_hubs = hub_rows.shape[0]
    outgoing = features[send_rows]
    received = lax.all_to_all(outgoing, "wide", split_axis=0, concat_axis=0, tiled=True).reshape(
        peers * slots, width
    )
    hub_features = lax.all_gather(features[hub_rows], ("wide", "narrow"), axis=0, tiled=True)
    buffer = jnp.concatenate([features, received, hub_features], axis=0)
    src_blocks = buffer.shape[0] // TILE
    dst_blocks = nodes // TILE
    buffer = buffer.reshape(src_blocks, TILE, width)
    live = tile_live.astype(jnp.float32)[:, None, None]
    picked = buffer[tile_src]
    products = (
        jnp.einsum("tij,tjf->tif", tile_weights, picked, preferred_element_type=jnp.float32) * live
    )
    aggregate = (
        jax.ops.segment_sum(products, tile_dst, num_segments=dst_blocks)
        .reshape(nodes, width)
        .astype(jnp.bfloat16)
    )
    pre = (
        jnp.dot(features, w_self, preferred_element_type=jnp.float32)
        + jnp.dot(aggregate, w_neigh, preferred_element_type=jnp.float32)
        + bias
    )
    hidden = gelu_tanh(pre).astype(jnp.bfloat16)
    _, pullback = jax.vjp(gelu_tanh, pre)
    grad_pre = pullback(cotangent.astype(jnp.float32))[0].astype(jnp.bfloat16)
    part_self = jnp.dot(features.T, grad_pre, preferred_element_type=jnp.float32)
    part_neigh = jnp.dot(aggregate.T, grad_pre, preferred_element_type=jnp.float32)
    part_bias = jnp.sum(grad_pre.astype(jnp.float32), axis=0)
    grad_self, grad_neigh, grad_bias = lax.psum(
        (part_self, part_neigh, part_bias), ("wide", "narrow")
    )
    grad_agg = jnp.dot(grad_pre, w_neigh.T, preferred_element_type=jnp.float32).astype(jnp.bfloat16)
    back = (
        jnp.einsum(
            "tij,tif->tjf",
            tile_weights,
            grad_agg.reshape(dst_blocks, TILE, width)[tile_dst],
            preferred_element_type=jnp.float32,
        )
        * live
    )
    grad_buffer = jax.ops.segment_sum(back, tile_src, num_segments=src_blocks).reshape(
        src_blocks * TILE, width
    )
    grad_features = (
        jnp.dot(grad_pre, w_self.T, preferred_element_type=jnp.float32) + grad_buffer[:nodes]
    )
    bound = grad_buffer[nodes : nodes + peers * slots].reshape(peers, slots, width)
    hub_part = grad_buffer[nodes + peers * slots :]
    returned = lax.all_to_all(
        bound.astype(jnp.bfloat16), "wide", split_axis=0, concat_axis=0, tiled=True
    ).astype(bound.dtype)
    grad_features = grad_features.at[send_rows.reshape(-1)].add(returned.reshape(-1, width))
    summed = lax.psum(hub_part, ("wide", "narrow"))
    start = lax.axis_index(("wide", "narrow")) * owned_hubs
    mine = lax.dynamic_slice_in_dim(summed, start, owned_hubs, 0)
    grad_features = grad_features.at[hub_rows].add(mine)
    return (hidden, grad_features, grad_self, grad_neigh, grad_bias)


def solution(mesh):
    placed = (
        P(("wide", "narrow"), None),
        P(("wide", "narrow"), None),
        P(),
        P(),
        P(),
        P(("wide", "narrow"), None, None),
        P(("wide", "narrow")),
        P(("wide", "narrow")),
        P(("wide", "narrow")),
        P(("wide", "narrow"), None),
        P(("wide", "narrow")),
    )
    return jax.shard_map(
        on_device,
        mesh=mesh,
        in_specs=placed,
        out_specs=(P(("wide", "narrow"), None), P(("wide", "narrow"), None), P(), P(), P()),
        check_vma=False,
    )
```

profile of v0, /device:TPU:1, one launch (start us, length us, event | category | flops | bytes accessed | tf_op | source)
XLA Modules:
  0.0 655.8 jit_solution(1251056573524552303)
XLA Ops:
  7.2 0.8 compare_select_fusion
  8.1 5.4 gather_fusion
  13.5 9.8 %all-to-all-start = ((bf16[32,32,128]{2,1,0:T(8,128)(2,1)}), bf16[32,32,128]{2,1,0:T(8,128)(2,1)S(1)}, u32[]{:S(2)}, u32[]{:S(2)}) async-start(bf16[32,32,128]{2,1,0:T(8,128)(2,1)} %bitcast), calls=%async_computation | async-start | bytes 524288 | tf_op jit(solution)/shard_map/all_to_all | solution.py:32
  23.4 1.4 reshape.70
  26.0 1.9 gather_fusion.1
  27.9 179.0 %all-gather = bf16[1024,128]{1,0:T(8,128)(2,1)S(1)} all-gather(bf16[8,128]{1,0:T(8,128)(2,1)S(1)} %gather_fusion.1), channel_id=2, replica_groups=mesh['wide'=32,'narrow'=4] {'wide','narrow'}, dimensions={0}, use_global_device_ids=true | all-gather | bytes 264192 | tf_op jit(solution)/shard_map/all_gather | solution.py:35
  206.8 0.7 compare_select_fusion.3
  208.2 0.7 compare_select_fusion.2
  208.9 3.5 fusion.16
  212.5 14.1 %gather_fusion.2 = bf16[512,128,128]{2,1,0:T(8,128)(2,1)} fusion(bf16[48,128,128]{2,1,0:T(8,128)(2,1)S(1)} %bitcast.34, s32[1024]{0:T(1024)S(1)} %pad_clamp_fusion.1), kind=kCustom, calls=%fused_computation.2 | custom fusion | bytes 33556480 | tf_op jit(solution)/shard_map/gather | solution.py:41
  226.6 25.4 %multiply_bitcast_fusion.1 = f32[512,128,128]{1,2,0:T(8,128)} fusion(f32[512]{0:T(512)S(1)} %convert_element_type.29, bf16[512,128,128]{2,1,0:T(8,128)(2,1)} %gather_fusion.2, bf16[512,128,128]{2,1,0:T(8,128)(2,1)} %param.16), kind=kOutput, calls=%fused_computation.9 | convolution fusion | flops 2155872256 | bytes 67110912 | tf_op jit(solution)/shard_map/tij,tjf->tif/dot_general | solution.py:43
  252.0 33.4 %copy.20 = f32[512,128,128]{2,1,0:T(8,128)} copy(f32[512,128,128]{1,2,0:T(8,128)} %multiply_bitcast_fusion.1) | data formatting | bytes 67108864 | tf_op jit(solution)/shard_map/mul | solution.py:43
  285.7 66.1 %scatter_fusion = f32[32,128,128]{2,1,0:T(8,128)S(1)} fusion(f32[32,128,128]{2,1,0:T(8,128)S(1)} %broadcast_in_dim.28, s32[512]{0:T(512)S(1)} %copy-done.7, f32[512,128,128]{2,1,0:T(8,128)} %copy.20), kind=kCustom, calls=%fused_computation.4 | custom fusion | flops 8388608 | bytes 100665344 | tf_op jit(solution)/shard_map/scatter-add | solution.py:46
  352.0 6.9 %convert_reduce_fusion = (f32[256]{0:T(256)S(1)}, bf16[4096,256]{1,0:T(8,128)(2,1)S(1)}, bf16[4096,256]{1,0:T(8,128)(2,1)}) fusion(bf16[4096,256]{1,0:T(8,128)(2,1)} %param.12, f32[256]{0:T(256)S(1)} %copy-done.10, f32[4096,256]{1,0:T(8,128)} %fusion.16, bf16[4096,128]{1,0:T(8,128)(2,1)S(1)} %bitcast.36, bf16[128,256]{1,0:T(8,128)(2,1)S(1)} %copy-done), kind=kOutput, calls=%fused_computation.28 | convolution fusion | flops 296746752 | bytes 11601920 | tf_op jit(solution)/shard_map/dot_general | solution.py:52
  358.9 0.7 convolution_convert_fusion
  359.6 1.2 fusion.17
  360.8 1.4 convolution_bitcast_fusion
  362.2 14.1 %gather_fusion.3 = bf16[512,128,128]{2,1,0:T(8,128)(2,1)} fusion(bf16[32,128,128]{2,1,0:T(8,128)(2,1)S(1)} %bitcast.33, s32[1024]{0:T(1024)S(1)} %pad_clamp_fusion), kind=kCustom, calls=%fused_computation.3 | custom fusion | bytes 33556480 | tf_op jit(solution)/shard_map/gather | solution.py:69
  376.3 25.7 %multiply_bitcast_fusion = f32[512,128,128]{1,2,0:T(8,128)} fusion(f32[512]{0:T(512)S(1)} %convert_element_type.29, bf16[512,128,128]{2,1,0:T(8,128)(2,1)} %gather_fusion.3, bf16[512,128,128]{2,1,0:T(8,128)(2,1)} %param.16), kind=kOutput, calls=%fused_computation.8 | convolution fusion | flops 2155872256 | bytes 67110912 | tf_op jit(solution)/shard_map/tij,tif->tjf/dot_general | solution.py:66
  402.0 33.4 %copy.22 = f32[512,128,128]{2,1,0:T(8,128)} copy(f32[512,128,128]{1,2,0:T(8,128)} %multiply_bitcast_fusion) | data formatting | bytes 67108864 | tf_op jit(solution)/shard_map/mul | solution.py:66
  435.8 66.1 %scatter_fusion.1 = f32[48,128,128]{2,1,0:T(8,128)S(1)} fusion(f32[48,128,128]{2,1,0:T(8,128)S(1)} %broadcast_in_dim.33, s32[512]{0:T(512)S(1)} %copy-done.8, f32[512,128,128]{2,1,0:T(8,128)} %copy.22), kind=kCustom, calls=%fused_computation.5 | custom fusion | flops 8388608 | bytes 100665344 | tf_op jit(solution)/shard_map/scatter-add | solution.py:74
  502.0 0.8 slice.32
  502.9 1.5 slice.30
  504.4 0.7 slice.34
  505.1 3.9 all-to-all-start.1
  509.0 65.7 %psum.31 = f32[256]{0:T(256)} all-reduce(f32[256]{0:T(256)S(1)} %get-tuple-element.18), channel_id=1, replica_groups=mesh['wide'=32,'narrow'=4] {'wide','narrow'}, use_global_device_ids=true, to_apply=%region_8.0 | all-reduce | flops 256 | bytes 2048 | tf_op jit(solution)/shard_map/psum | solution.py:61
  574.6 3.0 convolution_add_fusion.1
  577.6 6.8 %scatter_custom_fusion.2 = f32[4096,128]{1,0:T(8,128)S(1)} fusion(f32[4096,128]{1,0:T(8,128)S(1)} %convolution_add_fusion.1, s32[1024]{0:T(1024)S(1)} %bitcast.41, bf16[1024,128]{1,0:T(8,128)(2,1)S(1)} %bitcast.40), kind=kCustom, calls=%fused_computation.33 | custom fusion | flops 262144 | bytes 2359296 | tf_op jit(solution)/shard_map/scatter-add | solution.py:85
  584.5 59.5 %all-reduce.3.cloned.1.call-done = (f32[1024,128]{1,0:T(8,128)}, f32[128,256]{0,1:T(8,128)}, f32[128,256]{1,0:T(8,128)}) async-done(((f32[1024,128]{1,0:T(8,128)}, f32[128,256]{0,1:T(8,128)}, f32[128,256]{1,0:T(8,128)}), (f32[1024,128]{1,0:T(8,128)}, f32[128,256]{0,1:T(8,128)}, f32[128,256]{1,0:T(8,128)})) %all-reduce.3.cloned.1.call-update) | async-done | bytes 786448 | tf_op jit(solution)/shard_map/psum | solution.py:86
  644.0 1.7 copy.23
  645.7 1.5 scatter_custom_fusion.3
  647.2 1.7 copy.33
  (38 shorter events, 2.9 us)
Async XLA Ops:
  7.2 344.8 %copy-start = (bf16[128,256]{1,0:T(8,128)(2,1)S(1)}, bf16[128,256]{1,0:T(8,128)(2,1)}, u32[]{:S(2)}) copy-start(bf16[128,256]{1,0:T(8,128)(2,1)} %param.14) | copy-start | bytes 196612
  7.2 201.7 %copy-start.3 = (bf16[4096,128]{1,0:T(8,128)(2,1)S(1)}, bf16[4096,128]{1,0:T(8,128)(2,1)}, u32[]{:S(2)}) copy-start(bf16[4096,128]{1,0:T(8,128)(2,1)} %param.11) | copy-start | bytes 3145732
  13.5 198.9 %all-to-all-start = ((bf16[32,32,128]{2,1,0:T(8,128)(2,1)}), bf16[32,32,128]{2,1,0:T(8,128)(2,1)S(1)}, u32[]{:S(2)}, u32[]{:S(2)}) async-start(bf16[32,32,128]{2,1,0:T(8,128)(2,1)} %bitcast), calls=%async_computation | async-start | bytes 524288 | tf_op jit(solution)/shard_map/all_to_all | solution.py:32
  23.4 620.7 %all-reduce.3.cloned.1.call-start = ((), (), s32[]{:S(2)}) async-start(), calls=%async_computation.2 | async-start | bytes 1572864 | tf_op jit(solution)/shard_map/psum | solution.py:86
  25.4 0.5 copy-start.9
  252.0 33.7 %copy-start.7 = (s32[512]{0:T(512)S(1)}, s32[512]{0:T(512)}, u32[]{:S(2)}) copy-start(s32[512]{0:T(512)} %param.18) | copy-start | bytes 6148
  285.7 66.3 %copy-start.10 = (f32[256]{0:T(256)S(1)}, f32[256]{0:T(256)}, u32[]{:S(2)}) copy-start(f32[256]{0:T(256)} %param.15) | copy-start | bytes 3076
  358.9 1.9 copy-start.2
  402.0 33.8 %copy-start.8 = (s32[512]{0:T(512)S(1)}, s32[512]{0:T(512)}, u32[]{:S(2)}) copy-start(s32[512]{0:T(512)} %param.17) | copy-start | bytes 6148
  435.8 67.0 %copy-start.6 = (s32[1024,1]{0,1:T(1,128)S(1)}, s32[1024,1]{0,1:T(1,128)}, u32[]{:S(2)}) copy-start(s32[1024,1]{0,1:T(1,128)} %reshape.70) | copy-start | bytes 12292
  502.0 72.7 %copy-start.5 = (bf16[128,256]{1,0:T(8,128)(2,1)S(1)}, bf16[128,256]{1,0:T(8,128)(2,1)}, u32[]{:S(2)}) copy-start(bf16[128,256]{1,0:T(8,128)(2,1)} %param.13) | copy-start | bytes 196612
  505.1 72.5 %all-to-all-start.1 = ((bf16[32,32,128]{2,1,0:T(8,128)(2,1)}), bf16[32,32,128]{2,1,0:T(8,128)(2,1)S(1)}, u32[]{:S(2)}, u32[]{:S(2)}) async-start(bf16[32,32,128]{2,1,0:T(8,128)(2,1)} %bitcast.9), calls=%async_computation.1 | async-start | bytes 524288 | tf_op jit(solution)/shard_map/all_to_all | solution.py:82
  574.6 74.3 %copy-start.1 = (bf16[128,256]{1,0:T(8,128)(2,1)S(1)}, bf16[128,256]{1,0:T(8,128)(2,1)}, u32[]{:S(2)}) copy-start(bf16[128,256]{1,0:T(8,128)(2,1)} %param.14) | copy-start | bytes 196612
  647.2 1.7 copy-start.4
Sparse Core Ops, SparseCore 0:
  503.0 140.9 all-reduce.2
where the time goes:
time: 660 us; the launch traced here: 656 us
  blocking collectives  245 us (37%)
  other arithmetic  144 us (22%)
  local copies, waits for them, and re-layouts  111 us (17%)
  matrix products  67.8 us (10%)
  waiting for transfers between devices  59.6 us (9%)
  between operations  14.2 us (2%)
  starting transfers between devices  13.7 us (2%)
    all_gather x1, blocking collectives, on_device(): lax.all_gather(features[hub_rows], ('wide', 'narrow'), axis=0, tiled=True)  179 us
    scatter-add x1, other arithmetic, on_device(): jax.ops.segment_sum(back, tile_src, num_segments=src_blocks)  66.1 us
    scatter-add x1, other arithmetic, on_device(): jax.ops.segment_sum(products, tile_dst, num_segments=dst_blocks)  66.1 us
    psum x1, blocking collectives, on_device(): lax.psum((part_self, part_neigh, part_bias), ('wide', 'narrow'))  65.7 us
    psum x1, waiting for transfers between devices, on_device(): summed = lax.psum(hub_part, ('wide', 'narrow'))  59.5 us
    mul x1, local copies, waits for them, and re-layouts, on_device(): jnp.einsum('tij,tjf->tif', tile_weights, picked, preferred_element_type=j...  33.4 us
    mul x1, local copies, waits for them, and re-layouts, on_device(): jnp.einsum('tij,tif->tjf', tile_weights, grad_agg.reshape(dst_blocks, TIL...  33.4 us
    dot_general x1, matrix products, on_device(): jnp.einsum('tij,tif->tjf', tile_weights, grad_agg.reshape(dst_blocks, TIL...  25.7 us
  transfers between devices with their start and end apart: 3, of which 1 were waited for; matrix products, arithmetic and copies ran while one was open for 3% of the time, Pallas kernels for 0%

commit v1 on v0

v1 whole, which is shorter than its diff:
```python
import functools

import jax
import jax.numpy as jnp
from jax import lax
from jax.experimental import pallas as pl
from jax.experimental.pallas import tpu as pltpu
from jax.sharding import PartitionSpec as P

MESH = pl.DeviceIdType.MESH
BF, F32, I32 = jnp.bfloat16, jnp.float32, jnp.int32
TILE = 128
DST = 32
SRC = 48
TILES = 512
SLOTS = 640
UNROLL = 16
ROWS = 1024
CHUNKS = 8
SLOT = 32
HUB = 8
WIDE = 32
NARROW = 4
GELU_A = 0.7978845608028654
GELU_B = 0.044715


def mm(a, b):
    return jnp.dot(a, b, preferred_element_type=F32)


def nt(a, b):
    return lax.dot_general(a, b, (((1,), (1,)), ((), ())), preferred_element_type=F32)


def tn(a, b):
    return lax.dot_general(a, b, (((0,), (0,)), ((), ())), preferred_element_type=F32)


def iota(shape, dim):
    return lax.broadcasted_iota(I32, shape, dim)


def tile_list(key, other, live, keys, zero):
    groups = 64
    hot = jnp.where((iota((groups, TILES), 0) == key) & (live > 0), 1.0, 0.0)
    before = jnp.where(iota((TILES, TILES), 0) < iota((TILES, TILES), 1), 1.0, 0.0).astype(BF)
    rank = mm(hot.astype(BF), before)
    count = jnp.sum(hot, axis=1, keepdims=True).astype(I32)
    even = ((count + 1) // 2 * 2).astype(F32)
    lower = jnp.where(iota((groups, groups), 1) < iota((groups, groups), 0), 1.0, 0.0).astype(BF)
    start = mm(lower, jnp.broadcast_to(even, (groups, TILE)).astype(BF))[:, :1]
    total = jnp.sum(even, axis=0, keepdims=True)
    place = jnp.sum(hot * (rank + start), axis=0, keepdims=True).astype(I32)
    place = jnp.where(live > 0, place, -1)
    at = jnp.where(iota((SLOTS, TILES), 0) == place, 1.0, 0.0).astype(BF)
    t = iota((1, TILES), 1)
    rows = [t // 16, t % 16, other - zero, key - keys]
    row = iota((8, TILES), 0)
    values = jnp.zeros((8, TILES), I32)
    for r, v in enumerate(rows):
        values = jnp.where(row == r, v, values)
    got = nt(values.astype(F32).astype(BF), at).astype(I32)
    pairs = (total * 0.5).astype(I32)
    out = jnp.concatenate(
        [
            got[0:1] * 16 + got[1:2],
            got[2:3] + zero,
            got[3:4] + keys,
            jnp.broadcast_to(pairs, (1, SLOTS)),
        ],
        axis=0,
    )
    return jnp.concatenate([out, out], axis=0)


def fetch_kernel(
    send_rows, hub_rows, feat, src, dst, live, got, list_f, list_b,
    wide32, hubs, picked, msg, near, own, s_row, r_row, s_hub, r_hub, s_near, r_near, s_own,
):
    w = lax.axis_index("wide")
    n = lax.axis_index("narrow")
    barrier = pltpu.get_barrier_semaphore()

    def greet(o, c):
        pl.semaphore_signal(
            barrier, inc=1, device_id=(lax.rem(w + o, WIDE), n), device_id_type=MESH
        )
        return c

    lax.fori_loop(1, WIDE, greet, 0)
    for k in range(1, NARROW):
        pl.semaphore_signal(
            barrier, inc=1, device_id=(w, lax.rem(n + k, NARROW)), device_id_type=MESH
        )

    wide32[...] = feat[...].astype(F32)
    for j in range(HUB):
        hubs[pl.ds(j, 1), :] = wide32[pl.ds(hub_rows[j], 1), :]

    def pick(p, c):
        for j in range(SLOT):
            picked[pl.ds(p * SLOT + j, 1), :] = wide32[pl.ds(send_rows[p, j], 1), :]
        return c

    lax.fori_loop(0, WIDE, pick, 0)
    msg[...] = picked[...].astype(BF)
    near[n] = hubs[...]

    pl.semaphore_wait(barrier, WIDE - 1 + NARROW - 1)

    def near_copy(k, slot):
        return pltpu.make_async_remote_copy(
            src_ref=hubs,
            dst_ref=near.at[slot],
            send_sem=s_near.at[k],
            recv_sem=r_near.at[k],
            device_id=(w, lax.rem(n + k, NARROW)),
            device_id_type=MESH,
        )

    def row_copy(o, slot):
        p = lax.rem(w + o, WIDE)
        return pltpu.make_async_remote_copy(
            src_ref=msg.at[pl.ds(p * SLOT, SLOT)],
            dst_ref=got.at[slot, pl.ds(0, SLOT)],
            send_sem=s_row.at[o],
            recv_sem=r_row.at[o],
            device_id=(p, n),
            device_id_type=MESH,
        )

    def hub_copy(o, slot):
        return pltpu.make_async_remote_copy(
            src_ref=own,
            dst_ref=got.at[slot, pl.ds(SLOT, SLOT)],
            send_sem=s_hub.at[o],
            recv_sem=r_hub.at[o],
            device_id=(lax.rem(w + o, WIDE), n),
            device_id_type=MESH,
        )

    for k in range(1, NARROW):
        near_copy(k, n).start()

    def send_row(o, c):
        row_copy(o, w).start()
        return c

    lax.fori_loop(1, WIDE, send_row, 0)
    mine_row = pltpu.make_async_copy(
        msg.at[pl.ds(w * SLOT, SLOT)], got.at[w, pl.ds(0, SLOT)], s_own.at[0]
    )
    mine_row.start()
    for k in range(1, NARROW):
        near_copy(k, lax.rem(n + NARROW - k, NARROW)).wait_recv()
    own[...] = near[...].reshape(NARROW * HUB, TILE).astype(BF)

    def send_hub(o, c):
        hub_copy(o, w).start()
        return c

    lax.fori_loop(1, WIDE, send_hub, 0)
    mine_hub = pltpu.make_async_copy(own, got.at[w, pl.ds(SLOT, SLOT)], s_own.at[1])
    mine_hub.start()

    def flat(ref):
        return jnp.concatenate([ref[pl.ds(r, 1), :] for r in range(TILES // TILE)], axis=1)

    s, d, l = flat(src), flat(dst), flat(live)
    list_f[...] = tile_list(d, s, l, DST, SRC)
    list_b[...] = tile_list(s, d, l, SRC, DST)

    def finish(o, c):
        slot = lax.rem(w + WIDE - o, WIDE)
        row_copy(o, slot).wait()
        hub_copy(o, slot).wait()
        return c

    lax.fori_loop(1, WIDE, finish, 0)
    for k in range(1, NARROW):
        near_copy(k, n).wait_send()
    mine_row.wait()
    mine_hub.wait()


def fetch(feat, send_rows, hub_rows, src, dst, live):
    smem = pl.BlockSpec(memory_space=pltpu.SMEM)
    vmem = pl.BlockSpec(memory_space=pltpu.VMEM)
    dma = pltpu.SemaphoreType.DMA
    return pl.pallas_call(
        fetch_kernel,
        out_shape=(
            jax.ShapeDtypeStruct((WIDE, 2 * SLOT, TILE), BF),
            jax.ShapeDtypeStruct((8, SLOTS), I32),
            jax.ShapeDtypeStruct((8, SLOTS), I32),
        ),
        in_specs=[smem, smem, vmem, vmem, vmem, vmem],
        out_specs=(pl.BlockSpec(memory_space=pl.ANY), vmem, vmem),
        scratch_shapes=[
            pltpu.VMEM((DST * TILE, TILE), F32),
            pltpu.VMEM((HUB, TILE), F32),
            pltpu.VMEM((WIDE * SLOT, TILE), F32),
            pltpu.VMEM((WIDE * SLOT, TILE), BF),
            pltpu.VMEM((NARROW, HUB, TILE), F32),
            pltpu.VMEM((NARROW * HUB, TILE), BF),
            dma((WIDE,)), dma((WIDE,)), dma((WIDE,)), dma((WIDE,)),
            dma((NARROW,)), dma((NARROW,)), dma((2,)),
        ],
        compiler_params=pltpu.CompilerParams(
            collective_id=0, has_side_effects=True, vmem_limit_bytes=24 * 2**20
        ),
    )(send_rows, hub_rows, feat, src, dst, live)


def layer_kernel(
    list_f, list_b, feat, got, cot, w2, wt2, bias, tiles, hidden, gfeat, bound, msg,
    wbuf, buf, cotb, hidb, gfb, bnb, msb, agg, gt, gbt, wg, gb, sem_t, sem,
):
    quads = TILE // SLOT
    loads = [
        pltpu.make_async_copy(feat, buf.at[pl.ds(0, DST * quads)], sem.at[0]),
        pltpu.make_async_copy(
            got.at[:, pl.ds(0, SLOT)], buf.at[pl.ds(DST * quads, WIDE)], sem.at[1]
        ),
        pltpu.make_async_copy(
            got.at[:, pl.ds(SLOT, SLOT)], buf.at[pl.ds(DST * quads + WIDE, WIDE)], sem.at[2]
        ),
        pltpu.make_async_copy(cot, cotb, sem.at[3]),
    ]
    for c in loads[:3]:
        c.start()
    per = TILES // CHUNKS
    tile_loads = [
        pltpu.make_async_copy(
            tiles.at[pl.ds(i * per, per)], wbuf.at[pl.ds(i * per, per)], sem_t.at[i]
        )
        for i in range(CHUNKS)
    ]
    for c in tile_loads:
        c.start()
    loads[3].start()

    def clear(i, c):
        agg[i] = jnp.zeros((TILE, TILE), F32)
        return c

    lax.fori_loop(0, DST + 1, clear, 0)

    def clear_back(i, c):
        gbt[DST + i] = jnp.zeros((TILE, TILE), F32)
        return c

    lax.fori_loop(0, SRC - DST + 1, clear_back, 0)
    buf[pl.ds(SRC * quads, quads)] = jnp.zeros((quads, SLOT, TILE), BF)
    gt[DST] = jnp.zeros((TILE, TILE), BF)
    gb[...] = jnp.zeros_like(gb)
    wg[...] = jnp.zeros_like(wg)
    for c in loads[:3]:
        c.wait()
    for c in tile_loads:
        c.wait()

    def rows_of(s):
        return buf[pl.ds(s * quads, quads)].reshape(TILE, TILE)

    def forward(i, c):
        parts = []
        for u in range(UNROLL):
            k = 2 * (i * UNROLL + u)
            left = jnp.concatenate([wbuf[list_f[0, k]], wbuf[list_f[0, k + 1]]], axis=1)
            right = jnp.concatenate(
                [rows_of(list_f[1, k]), rows_of(list_f[1, k + 1])], axis=0
            )
            parts.append(mm(left, right))
        for u in range(UNROLL):
            agg[list_f[2, 2 * (i * UNROLL + u)]] += parts[u]
        return c

    lax.fori_loop(0, (list_f[3, 0] + UNROLL - 1) // UNROLL, forward, 0)
    loads[3].wait()
    blocks = ROWS // TILE

    def dense(i, c):
        rows = pl.ds(i * ROWS, ROWS)
        f = buf[pl.ds(i * blocks * quads, blocks * quads)].reshape(ROWS, TILE)
        a = agg[pl.ds(i * blocks, blocks)].reshape(ROWS, TILE).astype(BF)
        x = jnp.concatenate([f, a], axis=1)
        pre = mm(x, w2[...]) + bias[...]
        square = pre * pre
        t = jnp.tanh(pre * (GELU_A + (GELU_A * GELU_B) * square))
        half = 0.5 + 0.5 * t
        hidb[rows, :] = (pre * half).astype(BF)
        slope = half + pre * (0.5 - 0.5 * t * t) * (GELU_A + (3 * GELU_A * GELU_B) * square)
        gp = (cotb[rows, :].astype(F32) * slope).astype(BF)
        wg[...] += tn(x, gp)
        gb[...] += jnp.sum(gp.astype(F32).reshape(ROWS // 8, 8, 2 * TILE), axis=0)
        g2 = nt(wt2[...], gp)
        for j in range(blocks):
            gbt[i * blocks + j] = g2[:TILE, j * TILE : (j + 1) * TILE]
            gt[i * blocks + j] = g2[TILE:, j * TILE : (j + 1) * TILE].astype(BF)
        return c

    lax.fori_loop(0, DST // blocks, dense, 0)
    out_hidden = pltpu.make_async_copy(hidb, hidden, sem.at[4])
    out_hidden.start()

    def backward(i, c):
        parts = []
        for u in range(UNROLL):
            k = 2 * (i * UNROLL + u)
            left = jnp.concatenate([gt[list_b[1, k]], gt[list_b[1, k + 1]]], axis=1)
            right = jnp.concatenate([wbuf[list_b[0, k]], wbuf[list_b[0, k + 1]]], axis=0)
            parts.append(mm(left, right))
        for u in range(UNROLL):
            gbt[list_b[2, 2 * (i * UNROLL + u)]] += parts[u]
        return c

    lax.fori_loop(0, (list_b[3, 0] + UNROLL - 1) // UNROLL, backward, 0)

    def finish_own(i, c):
        gfb[i] = gbt[i].T
        return c

    lax.fori_loop(0, DST, finish_own, 0, unroll=4)
    out_own = pltpu.make_async_copy(gfb, gfeat, sem.at[5])
    out_own.start()
    bias_sum = jnp.sum(gb[...], axis=0, keepdims=True)
    row = iota((16, TILE), 0)
    bias_rows = jnp.where(
        row == 0, bias_sum[:, :TILE], jnp.where(row == 1, bias_sum[:, TILE:], 0.0)
    ).astype(BF)
    for i in range(WIDE * SLOT // TILE):
        bnb[pl.ds(i * quads, quads)] = gbt[DST + i].T.astype(BF).reshape(quads, SLOT, TILE)
        hub = gbt[DST + WIDE * SLOT // TILE + i].T.astype(BF).reshape(quads, SLOT, TILE)
        msb[pl.ds(i * quads, quads), pl.ds(0, SLOT), :] = hub
    for p in range(WIDE):
        part = wg[pl.ds(8 * p, 8), :]
        msb[p, pl.ds(SLOT, 16), :] = jnp.concatenate(
            [part[:, :TILE], part[:, TILE:]], axis=0
        ).astype(BF)
        msb[p, pl.ds(SLOT + 16, 16), :] = bias_rows
    outs = [
        pltpu.make_async_copy(bnb, bound, sem.at[6]),
        pltpu.make_async_copy(msb, msg, sem.at[7]),
    ]
    for c in outs:
        c.start()
    for c in outs:
        c.wait()
    out_own.wait()
    out_hidden.wait()


def layer(list_f, list_b, feat, got, cot, w2, wt2, bias, tiles):
    smem = pl.BlockSpec(memory_space=pltpu.SMEM)
    vmem = pl.BlockSpec(memory_space=pltpu.VMEM)
    hbm = pl.BlockSpec(memory_space=pl.ANY)
    dma = pltpu.SemaphoreType.DMA
    quads = TILE // SLOT
    return pl.pallas_call(
        layer_kernel,
        out_shape=(
            jax.ShapeDtypeStruct((DST * TILE, 2 * TILE), BF),
            jax.ShapeDtypeStruct((DST, TILE, TILE), F32),
            jax.ShapeDtypeStruct((WIDE, SLOT, TILE), BF),
            jax.ShapeDtypeStruct((WIDE, 2 * SLOT, TILE), BF),
        ),
        in_specs=[smem, smem, hbm, hbm, hbm, vmem, vmem, vmem, hbm],
        out_specs=(hbm, hbm, hbm, hbm),
        scratch_shapes=[
            pltpu.VMEM((TILES, TILE, TILE), BF),
            pltpu.VMEM(((SRC + 1) * quads, SLOT, TILE), BF),
            pltpu.VMEM((DST * TILE, 2 * TILE), BF),
            pltpu.VMEM((DST * TILE, 2 * TILE), BF),
            pltpu.VMEM((DST, TILE, TILE), F32),
            pltpu.VMEM((WIDE, SLOT, TILE), BF),
            pltpu.VMEM((WIDE, 2 * SLOT, TILE), BF),
            pltpu.VMEM((DST + 1, TILE, TILE), F32),
            pltpu.VMEM((DST + 1, TILE, TILE), BF),
            pltpu.VMEM((SRC + 1, TILE, TILE), F32),
            pltpu.VMEM((2 * TILE, 2 * TILE), F32),
            pltpu.VMEM((8, 2 * TILE), F32),
            dma((CHUNKS,)),
            dma((8,)),
        ],
        compiler_params=pltpu.CompilerParams(vmem_limit_bytes=60 * 2**20),
    )(list_f, list_b, feat, got, cot, w2, wt2, bias, tiles)


def reduce_kernel(
    hub_rows, rows, bound, msg, own, gfeat, g_self, g_neigh, g_bias,
    acc, back, sums, near_out, near_in, part, whole,
    s_back, r_back, s_sum, r_sum, s_near, r_near, s_part, r_part, s_own, s_out,
):
    w = lax.axis_index("wide")
    n = lax.axis_index("narrow")
    barrier = pltpu.get_barrier_semaphore()

    def greet(o, c):
        pl.semaphore_signal(
            barrier, inc=1, device_id=(lax.rem(w + o, WIDE), n), device_id_type=MESH
        )
        return c

    lax.fori_loop(1, WIDE, greet, 0)
    for k in range(1, NARROW):
        pl.semaphore_signal(
            barrier, inc=1, device_id=(w, lax.rem(n + k, NARROW)), device_id_type=MESH
        )
    load = pltpu.make_async_copy(own, acc, s_own.at[0])
    load.start()
    mine_sum = pltpu.make_async_copy(msg.at[w], sums.at[w], s_own.at[1])
    mine_sum.start()
    mine_back = pltpu.make_async_copy(bound.at[w], back.at[w], s_own.at[2])
    mine_back.start()
    pl.semaphore_wait(barrier, WIDE - 1 + NARROW - 1)

    def wide_copy(o, src, dst, send, recv):
        return pltpu.make_async_remote_copy(
            src_ref=src,
            dst_ref=dst,
            send_sem=send.at[o],
            recv_sem=recv.at[o],
            device_id=(lax.rem(w + o, WIDE), n),
            device_id_type=MESH,
        )

    def sum_copy(o, slot):
        return wide_copy(o, msg.at[lax.rem(w + o, WIDE)], sums.at[slot], s_sum, r_sum)

    def back_copy(o, slot):
        return wide_copy(o, bound.at[lax.rem(w + o, WIDE)], back.at[slot], s_back, r_back)

    def part_copy(o, slot):
        return wide_copy(o, part, whole.at[slot], s_part, r_part)

    def near_copy(k, slot):
        peer = lax.rem(n + k, NARROW)
        return pltpu.make_async_remote_copy(
            src_ref=near_out.at[peer],
            dst_ref=near_in.at[slot],
            send_sem=s_near.at[k],
            recv_sem=r_near.at[k],
            device_id=(w, peer),
            device_id_type=MESH,
        )

    def from_wide(o):
        return lax.rem(w + WIDE - o, WIDE)

    def send_sum(o, c):
        sum_copy(o, w).start()
        return c

    def send_back(o, c):
        back_copy(o, w).start()
        return c

    def send_part(o, c):
        part_copy(o, w).start()
        return c

    lax.fori_loop(1, WIDE, send_sum, 0)
    lax.fori_loop(1, WIDE, send_back, 0)

    def wait_sum(o, c):
        sum_copy(o, from_wide(o)).wait_recv()
        return c

    lax.fori_loop(1, WIDE, wait_sum, 0)
    mine_sum.wait()

    def add_up(q, total):
        return total + sums[q].astype(F32)

    total = lax.fori_loop(0, WIDE, add_up, jnp.zeros((2 * SLOT, TILE), F32))
    for k in range(NARROW):
        near_out[k] = jnp.concatenate([total[HUB * k : HUB * (k + 1)], total[SLOT : SLOT + 24]], 0)
    near_in[n] = near_out[n]
    for k in range(1, NARROW):
        near_copy(k, n).start()

    def wait_back(o, c):
        back_copy(o, from_wide(o)).wait_recv()
        return c

    lax.fori_loop(1, WIDE, wait_back, 0)
    mine_back.wait()
    for k in range(1, NARROW):
        near_copy(k, lax.rem(n + NARROW - k, NARROW)).wait_recv()
    near = near_in[0] + near_in[1] + near_in[2] + near_in[3]
    part[...] = near[HUB : HUB + 16]
    whole[w] = near[HUB : HUB + 16]
    lax.fori_loop(1, WIDE, send_part, 0)
    g_bias[...] = jnp.concatenate([near[24:25], near[25:26]], axis=1)

    high = near[0:HUB].astype(BF)
    low = (near[0:HUB] - high.astype(F32)).astype(BF)
    values = jnp.concatenate(
        [
            back[...].reshape(WIDE * SLOT, TILE),
            jnp.concatenate([high, low], axis=0),
            jnp.zeros((TILE - 2 * HUB, TILE), BF),
        ],
        axis=0,
    )
    lane = iota((1, TILE), 1)
    hub_at = jnp.full((1, TILE), -1, I32)
    for j in range(HUB):
        hub_at = jnp.where((lane == j) | (lane == j + HUB), hub_rows[j], hub_at)
    where = jnp.concatenate(
        [rows[pl.ds(r, 1), :] for r in range(WIDE * SLOT // TILE)] + [hub_at], axis=1
    )
    load.wait()
    step = 512
    span = where.shape[1]

    def scatter(i, c):
        at = pl.ds(i * step, step)
        hot = jnp.where(iota((step, span), 0) + i * step == where, 1.0, 0.0).astype(BF)
        acc[at, :] += mm(hot, values)
        return c

    lax.fori_loop(0, DST * TILE // step, scatter, 0)
    store = pltpu.make_async_copy(acc, gfeat, s_out.at[0])
    store.start()

    def wait_part(o, c):
        part_copy(o, from_wide(o)).wait_recv()
        return c

    lax.fori_loop(1, WIDE, wait_part, 0)
    for out, first in ((g_self, 0), (g_neigh, WIDE // 2)):
        for p in range(WIDE // 2):
            out[pl.ds(8 * p, 8), :] = jnp.concatenate(
                [whole[first + p, pl.ds(0, 8), :], whole[first + p, pl.ds(8, 8), :]], axis=1
            )

    def sent(o, c):
        sum_copy(o, w).wait_send()
        back_copy(o, w).wait_send()
        part_copy(o, w).wait_send()
        return c

    lax.fori_loop(1, WIDE, sent, 0)
    for k in range(1, NARROW):
        near_copy(k, n).wait_send()
    store.wait()


def reduce(hub_rows, rows, bound, msg, own):
    smem = pl.BlockSpec(memory_space=pltpu.SMEM)
    vmem = pl.BlockSpec(memory_space=pltpu.VMEM)
    hbm = pl.BlockSpec(memory_space=pl.ANY)
    dma = pltpu.SemaphoreType.DMA
    return pl.pallas_call(
        reduce_kernel,
        out_shape=(
            jax.ShapeDtypeStruct((DST * TILE, TILE), F32),
            jax.ShapeDtypeStruct((TILE, 2 * TILE), F32),
            jax.ShapeDtypeStruct((TILE, 2 * TILE), F32),
            jax.ShapeDtypeStruct((1, 2 * TILE), F32),
        ),
        in_specs=[smem, vmem, hbm, hbm, hbm],
        out_specs=(hbm, vmem, vmem, vmem),
        scratch_shapes=[
            pltpu.VMEM((DST * TILE, TILE), F32),
            pltpu.VMEM((WIDE, SLOT, TILE), BF),
            pltpu.VMEM((WIDE, 2 * SLOT, TILE), BF),
            pltpu.VMEM((NARROW, 32, TILE), F32),
            pltpu.VMEM((NARROW, 32, TILE), F32),
            pltpu.VMEM((16, TILE), F32),
            pltpu.VMEM((WIDE, 16, TILE), F32),
            dma((WIDE,)), dma((WIDE,)), dma((WIDE,)), dma((WIDE,)),
            dma((NARROW,)), dma((NARROW,)), dma((WIDE,)), dma((WIDE,)),
            dma((3,)), dma((1,)),
        ],
        compiler_params=pltpu.CompilerParams(
            collective_id=1, has_side_effects=True, vmem_limit_bytes=32 * 2**20
        ),
    )(hub_rows, rows, bound, msg, own)


def on_device(
    features, cotangent, w_self, w_neigh, bias, tile_weights, tile_src, tile_dst, tile_live,
    send_rows, hub_rows,
):
    quads = TILE // SLOT
    lanes = (TILES // TILE, TILE)
    got, list_f, list_b = fetch(
        features, send_rows, hub_rows,
        tile_src.reshape(lanes), tile_dst.reshape(lanes), tile_live.reshape(lanes),
    )
    w2 = jnp.concatenate([w_self, w_neigh], axis=0)
    hidden, own, bound, msg = layer(
        list_f, list_b, features.reshape(DST * quads, SLOT, TILE), got, cotangent,
        w2, w2, bias.reshape(1, 2 * TILE), tile_weights,
    )
    grad_features, grad_self, grad_neigh, grad_bias = reduce(
        hub_rows, send_rows.reshape(WIDE * SLOT // TILE, TILE), bound, msg,
        own.reshape(DST * TILE, TILE),
    )
    return (hidden, grad_features, grad_self, grad_neigh, grad_bias.reshape(2 * TILE))


def solution(mesh):
    both = ("wide", "narrow")
    placed = (
        P(both, None), P(both, None), P(), P(), P(), P(both, None, None),
        P(both), P(both), P(both), P(both, None), P(both),
    )
    return jax.shard_map(
        on_device,
        mesh=mesh,
        in_specs=placed,
        out_specs=(P(both, None), P(both, None), P(), P(), P()),
        check_vma=False,
    )
```

time: 660 us -> 90.5 us (0.14)
  blocking collectives: 245 us -> 0 us
  other arithmetic: 144 us -> 1.54 us
  local copies, waits for them, and re-layouts: 111 us -> 14.2 us
  Pallas kernels: 0 us -> 73.1 us
  matrix products: 67.8 us -> 0 us
  waiting for transfers between devices: 59.6 us -> 0 us
  starting transfers between devices: 13.7 us -> 0 us
  between operations: 14.2 us -> 0.69 us
    all_gather x1 -> x0, blocking collectives: 179 us -> none  [on_device(): lax.all_gather(features[hub_rows], ('wide', 'narrow'), axis=0, tiled=True)]
    scatter-add x4 -> x0, other arithmetic: 141 us -> none  [the longest x1 66.1 us: on_device(): jax.ops.segment_sum(back, tile_src, num_segments=src_blocks)]
    pallas_call x0 -> x3, Pallas kernels: none -> 73.1 us  [the longest x1 27.4 us: layer(): pl.pallas_call(layer_kernel, out_shape=(jax.ShapeDtypeStruct((DST * TILE,...]
    dot_general x8 -> x0, matrix products: 67.8 us -> none  [the longest x1 25.7 us: on_device(): jnp.einsum('tij,tif->tjf', tile_weights, grad_agg.reshape(dst_blocks, TIL...]
    mul x2 -> x0, local copies, waits for them, and re-layouts: 66.9 us -> none  [the longest x1 33.4 us: on_device(): jnp.einsum('tij,tjf->tif', tile_weights, picked, preferred_element_type=j...]
    psum x1 -> x0, blocking collectives: 65.7 us -> none  [on_device(): lax.psum((part_self, part_neigh, part_bias), ('wide', 'narrow'))]
    psum x1 -> x0, waiting for transfers between devices: 59.5 us -> none  [on_device(): summed = lax.psum(hub_part, ('wide', 'narrow'))]
    gather x4 -> x0, local copies, waits for them, and re-layouts: 35.5 us -> none  [the longest x1 14.1 us: on_device(): grad_agg.reshape(dst_blocks, TILE, width)[tile_dst]]
  transfers between devices with their start and end apart: 3 -> 0, of which waited for: 1 -> 0; matrix products, arithmetic and copies ran while one was open for 3% -> 0% of each run, Pallas kernels for 0% -> 0%
where the time goes in v1:
time: 90.5 us; the launch traced here: 89.5 us
  Pallas kernels  73.1 us (81%)
  local copies, waits for them, and re-layouts  14.2 us (16%)
  other arithmetic  1.54 us (2%)
    pallas_call x1, Pallas kernels, layer(): pl.pallas_call(layer_kernel, out_shape=(jax.ShapeDtypeStruct((DST * TILE,...  27.4 us
    pallas_call x1, Pallas kernels, reduce(): pl.pallas_call(reduce_kernel, out_shape=(jax.ShapeDtypeStruct((DST * TILE...  25.7 us
    pallas_call x1, Pallas kernels, fetch(): pl.pallas_call(fetch_kernel, out_shape=(jax.ShapeDtypeStruct((WIDE, 2 * S...  19.9 us
    unnamed x30, local copies, waits for them, and re-layouts  13.4 us

profile of v1, /device:TPU:1, one launch (start us, length us, event | category | flops | bytes accessed | tf_op | source)
XLA Modules:
  0.0 89.5 jit_solution(6951803025056639004)
XLA Ops:
  0.6 0.8 reshape.39.rows
  1.4 1.5 %pad_maximum_fusion.w2.wt2 = bf16[256,256]{1,0:T(8,128)(2,1)} fusion(bf16[128,256]{1,0:T(8,128)(2,1)} %param.14, bf16[128,256]{1,0:T(8,128)(2,1)} %param.13), kind=kLoop, calls=%fused_computation | loop fusion | flops 262144 | bytes 262144 | tf_op jit(solution)/shard_map/concatenate | solution.py:595
  3.0 0.0 copy-start
  3.0 1.2 %copy-done = bf16[4096,128]{1,0:T(8,128)(2,1)S(1)} copy-done((bf16[4096,128]{1,0:T(8,128)(2,1)S(1)}, bf16[4096,128]{1,0:T(8,128)(2,1)}, u32[]{:S(2)}) %copy-start) | copy-done | bytes 1048600
  4.2 0.0 copy-start.5
  4.2 0.7 copy-done.5
  4.9 0.0 copy-start.8
  4.9 0.7 copy-done.8
  5.6 0.0 copy-start.9
  5.6 0.7 copy-done.9
  6.3 0.0 copy-start.10
  6.3 0.7 copy-done.10
  6.9 0.0 copy-start.11
  6.9 0.7 copy-done.11
  7.6 19.9 %shard_map.146 = (bf16[32,64,128]{2,1,0:T(8,128)(2,1)S(1)}, s32[8,640]{1,0:T(8,128)S(1)}, s32[8,640]{1,0:T(8,128)S(1)}) custom-call(s32[32,32]{1,0:T(8,128)S(1)} %copy-done.5, s32[8]{0:T(128)S(1)} %copy-done.11, bf16[4096,128]{1,0:T(8,128)(2,1)S(1)} %copy-done, s32[4,128]{1,0:T(4,128)S(1)} %bitcast.9, s32[4,128]{1,0:T(4,128)S(1)} %bitcast.10, ...), custom_call_target="tpu_custom_call" | custom-call | tf_op jit(solution)/shard_map/pallas_call | solution.py:191
  27.5 0.0 copy-start.3
  27.5 0.8 copy-done.3
  28.3 0.0 copy-start.6
  28.3 0.6 copy-done.6
  28.9 0.0 copy-start.7
  28.9 0.6 copy-done.7
  29.5 27.4 %shard_map.147 = (bf16[4096,256]{1,0:T(8,128)(2,1)}, f32[32,128,128]{2,1,0:T(8,128)}, bf16[32,32,128]{2,1,0:T(8,128)(2,1)}, bf16[32,64,128]{2,1,0:T(8,128)(2,1)}) custom-call(s32[8,640]{1,0:T(8,128)} %copy-done.6, s32[8,640]{1,0:T(8,128)} %copy-done.7, bf16[128,32,128]{2,1,0:T(8,128)(2,1)} %bitcast.7, bf16[32,64,128]{2,1,0:T(8,128)(2,1)} %copy-done.3, ...), custom_call_target="tpu_custom_call" | custom-call | tf_op jit(solution)/shard_map/pallas_call | solution.py:361
  57.0 0.0 copy-done.12
  57.0 0.0 copy-start.1
  57.0 1.6 %copy-done.1 = f32[32,128,128]{2,1,0:T(8,128)S(1)} copy-done((f32[32,128,128]{2,1,0:T(8,128)S(1)}, f32[32,128,128]{2,1,0:T(8,128)}, u32[]{:S(2)}) %copy-start.1) | copy-done | bytes 2097176
  58.6 1.0 %copy-done.2 = bf16[32,64,128]{2,1,0:T(8,128)(2,1)S(1)} copy-done((bf16[32,64,128]{2,1,0:T(8,128)(2,1)S(1)}, bf16[32,64,128]{2,1,0:T(8,128)(2,1)}, u32[]{:S(2)}) %copy-start.2) | copy-done | bytes 524312
  59.6 0.9 %copy-done.4 = bf16[32,32,128]{2,1,0:T(8,128)(2,1)S(1)} copy-done((bf16[32,32,128]{2,1,0:T(8,128)(2,1)S(1)}, bf16[32,32,128]{2,1,0:T(8,128)(2,1)}, u32[]{:S(2)}) %copy-start.4) | copy-done | bytes 262168
  60.6 25.7 %shard_map.148 = (f32[4096,128]{1,0:T(8,128)S(1)}, f32[128,256]{1,0:T(8,128)S(1)}, f32[128,256]{1,0:T(8,128)S(1)}, f32[1,256]{1,0:T(1,128)S(1)}) custom-call(s32[8]{0:T(128)S(1)} %copy-done.12, s32[8,128]{1,0:T(8,128)S(1)} %reshape.39.rows, bf16[32,32,128]{2,1,0:T(8,128)(2,1)S(1)} %copy-done.4, bf16[32,64,128]{2,1,0:T(8,128)(2,1)S(1)} %copy-done.2, ...), custom_call_target="tpu_custom_call" | custom-call | tf_op jit(solution)/shard_map/pallas_call | solution.py:557
  86.3 1.3 %copy.20 = f32[4096,128]{1,0:T(8,128)} copy(f32[4096,128]{1,0:T(8,128)S(1)} %get-tuple-element.33) | data formatting | bytes 4194304
  87.6 0.7 copy.21
  88.3 0.7 copy.22
  88.9 0.6 copy.23
  (3 shorter events, 0.0 us)
Async XLA Ops:
  3.0 1.2 %copy-start = (bf16[4096,128]{1,0:T(8,128)(2,1)S(1)}, bf16[4096,128]{1,0:T(8,128)(2,1)}, u32[]{:S(2)}) copy-start(bf16[4096,128]{1,0:T(8,128)(2,1)} %feat.1) | copy-start | bytes 3145732
  4.2 0.7 copy-start.5
  4.9 0.7 copy-start.8
  5.6 0.7 copy-start.9
  6.3 0.7 copy-start.10
  6.9 0.7 copy-start.11
  27.5 0.8 copy-start.3
  28.3 0.6 copy-start.6
  28.9 0.6 copy-start.7
  29.5 27.5 %copy-start.12 = (s32[8]{0:T(128)S(1)}, s32[8]{0:T(128)}, u32[]{:S(2)}) copy-start(s32[8]{0:T(128)} %hub_rows.3) | copy-start | bytes 100
  57.0 1.6 %copy-start.1 = (f32[32,128,128]{2,1,0:T(8,128)S(1)}, f32[32,128,128]{2,1,0:T(8,128)}, u32[]{:S(2)}) copy-start(f32[32,128,128]{2,1,0:T(8,128)} %get-tuple-element.22) | copy-start | bytes 6291460
  58.6 1.0 %copy-start.2 = (bf16[32,64,128]{2,1,0:T(8,128)(2,1)S(1)}, bf16[32,64,128]{2,1,0:T(8,128)(2,1)}, u32[]{:S(2)}) copy-start(bf16[32,64,128]{2,1,0:T(8,128)(2,1)} %get-tuple-element.21.msg) | copy-start | bytes 1572868
  59.6 0.9 %copy-start.4 = (bf16[32,32,128]{2,1,0:T(8,128)(2,1)S(1)}, bf16[32,32,128]{2,1,0:T(8,128)(2,1)}, u32[]{:S(2)}) copy-start(bf16[32,32,128]{2,1,0:T(8,128)(2,1)} %get-tuple-element.20.bound) | copy-start | bytes 786436

commit v2 on v1

v2 whole, which is shorter than its diff:
```python
import functools

import jax
import jax.numpy as jnp
from jax import lax
from jax.experimental import pallas as pl
from jax.experimental.pallas import tpu as pltpu
from jax.sharding import PartitionSpec as P

MESH = pl.DeviceIdType.MESH
BF, F32, I32 = jnp.bfloat16, jnp.float32, jnp.int32
TILE = 128
DST = 32
SRC = 48
TILES = 512
SLOTS = 640
UNROLL = 16
ROWS = 1024
CHUNKS = 8
SLOT = 32
QUADS = TILE // SLOT
HUB = 8
WIDE = 32
NARROW = 4
GELU_A = 0.7978845608028654
GELU_B = 0.044715


def mm(a, b):
    return jnp.dot(a, b, preferred_element_type=F32)


def nt(a, b):
    return lax.dot_general(a, b, (((1,), (1,)), ((), ())), preferred_element_type=F32)


def tn(a, b):
    return lax.dot_general(a, b, (((0,), (0,)), ((), ())), preferred_element_type=F32)


def iota(shape, dim):
    return lax.broadcasted_iota(I32, shape, dim)


def tile_list(key, other, live, keys, zero):
    groups = 64
    hot = jnp.where((iota((groups, TILES), 0) == key) & (live > 0), 1.0, 0.0)
    before = jnp.where(iota((TILES, TILES), 0) < iota((TILES, TILES), 1), 1.0, 0.0).astype(BF)
    rank = mm(hot.astype(BF), before)
    count = jnp.sum(hot, axis=1, keepdims=True).astype(I32)
    even = ((count + 1) // 2 * 2).astype(F32)
    lower = jnp.where(iota((groups, groups), 1) < iota((groups, groups), 0), 1.0, 0.0).astype(BF)
    start = mm(lower, jnp.broadcast_to(even, (groups, TILE)).astype(BF))[:, :1]
    total = jnp.sum(even, axis=0, keepdims=True)
    place = jnp.sum(hot * (rank + start), axis=0, keepdims=True).astype(I32)
    place = jnp.where(live > 0, place, -1)
    at = jnp.where(iota((SLOTS, TILES), 0) == place, 1.0, 0.0).astype(BF)
    t = iota((1, TILES), 1)
    rows = [t // 16, t % 16, other - zero, key - keys]
    row = iota((8, TILES), 0)
    values = jnp.zeros((8, TILES), I32)
    for r, v in enumerate(rows):
        values = jnp.where(row == r, v, values)
    got = nt(values.astype(F32).astype(BF), at).astype(I32)
    pairs = (total * 0.5).astype(I32)
    out = jnp.concatenate(
        [
            got[0:1] * 16 + got[1:2],
            got[2:3] + zero,
            got[3:4] + keys,
            jnp.broadcast_to(pairs, (1, SLOTS)),
        ],
        axis=0,
    )
    return out


def greet_all(w, n):
    barrier = pltpu.get_barrier_semaphore()

    def greet(o, c):
        pl.semaphore_signal(
            barrier, inc=1, device_id=(lax.rem(w + o, WIDE), n), device_id_type=MESH
        )
        return c

    lax.fori_loop(1, WIDE, greet, 0)
    for k in range(1, NARROW):
        pl.semaphore_signal(
            barrier, inc=1, device_id=(w, lax.rem(n + k, NARROW)), device_id_type=MESH
        )
    return barrier


def fetch_kernel(
    feat, cot, w_self, w_neigh, bias, tiles, src, dst, live, send_rows, hub_rows,
    wbuf, buf, cotb, w2, b2, list_f, list_b,
    send_at, hub_at, keys, wide32, hubs, picked, msg, near, own, lists,
    s_row, r_row, s_hub, r_hub, s_near, r_near, s_own, s_in, s_big, s_list,
):
    w = lax.axis_index("wide")
    n = lax.axis_index("narrow")
    small = [
        pltpu.make_async_copy(send_rows, send_at, s_in.at[0]),
        pltpu.make_async_copy(hub_rows, hub_at, s_in.at[1]),
        pltpu.make_async_copy(feat, buf.at[pl.ds(0, DST * QUADS)], s_in.at[2]),
        pltpu.make_async_copy(src, keys.at[0], s_in.at[3]),
        pltpu.make_async_copy(dst, keys.at[1], s_in.at[4]),
        pltpu.make_async_copy(live, keys.at[2], s_in.at[5]),
    ]
    for c in small:
        c.start()
    barrier = greet_all(w, n)
    big = [
        pltpu.make_async_copy(w_self, w2.at[pl.ds(0, TILE)], s_big.at[0]),
        pltpu.make_async_copy(w_neigh, w2.at[pl.ds(TILE, TILE)], s_big.at[1]),
        pltpu.make_async_copy(bias, b2, s_big.at[2]),
        pltpu.make_async_copy(cot, cotb, s_big.at[3]),
    ]
    per = TILES // CHUNKS
    big += [
        pltpu.make_async_copy(
            tiles.at[pl.ds(i * per, per)], wbuf.at[pl.ds(i * per, per)], s_big.at[4 + i]
        )
        for i in range(CHUNKS)
    ]
    for c in big:
        c.start()
    buf[pl.ds(SRC * QUADS, QUADS)] = jnp.zeros((QUADS, SLOT, TILE), BF)
    for c in small[:3]:
        c.wait()
    wide32[...] = buf[pl.ds(0, DST * QUADS)].astype(F32).reshape(DST * TILE, TILE)
    for j in range(HUB):
        hubs[pl.ds(j, 1), :] = wide32[pl.ds(hub_at[j], 1), :]

    def pick(p, c):
        for j in range(SLOT):
            picked[pl.ds(p * SLOT + j, 1), :] = wide32[pl.ds(send_at[p, j], 1), :]
        return c

    lax.fori_loop(0, WIDE, pick, 0)
    msg[...] = picked[...].astype(BF).reshape(WIDE, SLOT, TILE)
    near[n] = hubs[...]

    pl.semaphore_wait(barrier, WIDE - 1 + NARROW - 1)
    rows_at, hubs_at = DST * QUADS, DST * QUADS + WIDE

    def near_copy(k, slot):
        return pltpu.make_async_remote_copy(
            src_ref=hubs,
            dst_ref=near.at[slot],
            send_sem=s_near.at[k],
            recv_sem=r_near.at[k],
            device_id=(w, lax.rem(n + k, NARROW)),
            device_id_type=MESH,
        )

    def row_copy(o, slot):
        p = lax.rem(w + o, WIDE)
        return pltpu.make_async_remote_copy(
            src_ref=msg.at[p],
            dst_ref=buf.at[rows_at + slot],
            send_sem=s_row.at[o],
            recv_sem=r_row.at[o],
            device_id=(p, n),
            device_id_type=MESH,
        )

    def hub_copy(o, slot):
        return pltpu.make_async_remote_copy(
            src_ref=own,
            dst_ref=buf.at[hubs_at + slot],
            send_sem=s_hub.at[o],
            recv_sem=r_hub.at[o],
            device_id=(lax.rem(w + o, WIDE), n),
            device_id_type=MESH,
        )

    for k in range(1, NARROW):
        near_copy(k, n).start()

    def send_row(o, c):
        row_copy(o, w).start()
        return c

    lax.fori_loop(1, WIDE, send_row, 0)
    mine_row = pltpu.make_async_copy(msg.at[w], buf.at[rows_at + w], s_own.at[0])
    mine_row.start()
    for k in range(1, NARROW):
        near_copy(k, lax.rem(n + NARROW - k, NARROW)).wait_recv()
    own[...] = near[...].reshape(NARROW * HUB, TILE).astype(BF)

    def send_hub(o, c):
        hub_copy(o, w).start()
        return c

    lax.fori_loop(1, WIDE, send_hub, 0)
    mine_hub = pltpu.make_async_copy(own, buf.at[hubs_at + w], s_own.at[1])
    mine_hub.start()

    for c in small[3:]:
        c.wait()

    def flat(i):
        return jnp.concatenate([keys[i, pl.ds(r, 1), :] for r in range(TILES // TILE)], axis=1)

    s, d, l = flat(0), flat(1), flat(2)
    lists[0] = tile_list(d, s, l, DST, SRC)
    lists[1] = tile_list(s, d, l, SRC, DST)
    out_lists = [
        pltpu.make_async_copy(lists.at[0], list_f, s_list.at[0]),
        pltpu.make_async_copy(lists.at[1], list_b, s_list.at[1]),
    ]
    for c in out_lists:
        c.start()

    def finish(o, c):
        slot = lax.rem(w + WIDE - o, WIDE)
        row_copy(o, slot).wait()
        hub_copy(o, slot).wait()
        return c

    lax.fori_loop(1, WIDE, finish, 0)
    for k in range(1, NARROW):
        near_copy(k, n).wait_send()
    mine_row.wait()
    mine_hub.wait()
    for c in out_lists:
        c.wait()
    for c in big:
        c.wait()


def in_vmem(x):
    return pltpu.with_memory_space_constraint(x, pltpu.VMEM)


def in_hbm(x):
    return pltpu.with_memory_space_constraint(x, pltpu.HBM)


def fetch(feat, cot, w_self, w_neigh, bias, tiles, src, dst, live, send_rows, hub_rows):
    vmem = pl.BlockSpec(memory_space=pltpu.VMEM)
    hbm = pl.BlockSpec(memory_space=pltpu.HBM)
    dma = pltpu.SemaphoreType.DMA
    return pl.pallas_call(
        fetch_kernel,
        out_shape=(
            pltpu.VMEM((TILES, TILE, TILE), BF),
            pltpu.VMEM(((SRC + 1) * QUADS, SLOT, TILE), BF),
            pltpu.VMEM((DST * TILE, 2 * TILE), BF),
            pltpu.VMEM((2 * TILE, 2 * TILE), BF),
            pltpu.VMEM((1, 2 * TILE), F32),
            pltpu.HBM((4, SLOTS), I32),
            pltpu.HBM((4, SLOTS), I32),
        ),
        in_specs=[hbm] * 11,
        out_specs=(vmem, vmem, vmem, vmem, vmem, hbm, hbm),
        scratch_shapes=[
            pltpu.SMEM((WIDE, SLOT), I32),
            pltpu.SMEM((HUB,), I32),
            pltpu.VMEM((3, TILES // TILE, TILE), I32),
            pltpu.VMEM((DST * TILE, TILE), F32),
            pltpu.VMEM((HUB, TILE), F32),
            pltpu.VMEM((WIDE * SLOT, TILE), F32),
            pltpu.VMEM((WIDE, SLOT, TILE), BF),
            pltpu.VMEM((NARROW, HUB, TILE), F32),
            pltpu.VMEM((NARROW * HUB, TILE), BF),
            pltpu.VMEM((2, 4, SLOTS), I32),
            dma((WIDE,)), dma((WIDE,)), dma((WIDE,)), dma((WIDE,)),
            dma((NARROW,)), dma((NARROW,)), dma((2,)), dma((6,)), dma((4 + CHUNKS,)), dma((2,)),
        ],
        compiler_params=pltpu.CompilerParams(
            collective_id=0, has_side_effects=True, vmem_limit_bytes=30 * 2**20
        ),
    )(
        *map(in_hbm, (feat, cot, w_self, w_neigh, bias, tiles, src, dst, live, send_rows, hub_rows))
    )


def layer_kernel(
    lists_f, lists_b, wbuf, buf, cotb, w2, bias, hidden, own, bound, sums, hubs,
    list_f, list_b, hidb, agg, gt, gbt, wg, gb, sem,
):
    loads = [
        pltpu.make_async_copy(lists_f, list_f, sem.at[0]),
        pltpu.make_async_copy(lists_b, list_b, sem.at[1]),
    ]
    for c in loads:
        c.start()

    def clear(i, c):
        agg[i] = jnp.zeros((TILE, TILE), F32)
        return c

    lax.fori_loop(0, DST + 1, clear, 0)

    def clear_back(i, c):
        gbt[DST + i] = jnp.zeros((TILE, TILE), F32)
        return c

    lax.fori_loop(0, SRC - DST + 1, clear_back, 0)
    gt[DST] = jnp.zeros((TILE, TILE), BF)
    gb[...] = jnp.zeros_like(gb)
    wg[...] = jnp.zeros_like(wg)
    for c in loads:
        c.wait()

    def rows_of(s):
        return buf[pl.ds(s * QUADS, QUADS)].reshape(TILE, TILE)

    def forward(i, c):
        parts = []
        for u in range(UNROLL):
            k = 2 * (i * UNROLL + u)
            left = jnp.concatenate([wbuf[list_f[0, k]], wbuf[list_f[0, k + 1]]], axis=1)
            right = jnp.concatenate(
                [rows_of(list_f[1, k]), rows_of(list_f[1, k + 1])], axis=0
            )
            parts.append(mm(left, right))
        for u in range(UNROLL):
            agg[list_f[2, 2 * (i * UNROLL + u)]] += parts[u]
        return c

    lax.fori_loop(0, (list_f[3, 0] + UNROLL - 1) // UNROLL, forward, 0)
    blocks = ROWS // TILE

    def dense(i, c):
        rows = pl.ds(i * ROWS, ROWS)
        f = buf[pl.ds(i * blocks * QUADS, blocks * QUADS)].reshape(ROWS, TILE)
        a = agg[pl.ds(i * blocks, blocks)].reshape(ROWS, TILE).astype(BF)
        x = jnp.concatenate([f, a], axis=1)
        pre = mm(x, w2[...]) + bias[...]
        square = pre * pre
        t = jnp.tanh(pre * (GELU_A + (GELU_A * GELU_B) * square))
        half = 0.5 + 0.5 * t
        hidb[rows, :] = (pre * half).astype(BF)
        slope = half + pre * (0.5 - 0.5 * t * t) * (GELU_A + (3 * GELU_A * GELU_B) * square)
        gp = (cotb[rows, :].astype(F32) * slope).astype(BF)
        wg[...] += tn(x, gp)
        gb[...] += jnp.sum(gp.astype(F32).reshape(ROWS // 8, 8, 2 * TILE), axis=0)
        g2 = nt(w2[...], gp)
        for j in range(blocks):
            gbt[i * blocks + j] = g2[:TILE, j * TILE : (j + 1) * TILE]
            gt[i * blocks + j] = g2[TILE:, j * TILE : (j + 1) * TILE].astype(BF)
        return c

    lax.fori_loop(0, DST // blocks, dense, 0)
    out_hidden = pltpu.make_async_copy(hidb, hidden, sem.at[2])
    out_hidden.start()

    def backward(i, c):
        parts = []
        for u in range(UNROLL):
            k = 2 * (i * UNROLL + u)
            left = jnp.concatenate([gt[list_b[1, k]], gt[list_b[1, k + 1]]], axis=1)
            right = jnp.concatenate([wbuf[list_b[0, k]], wbuf[list_b[0, k + 1]]], axis=0)
            parts.append(mm(left, right))
        for u in range(UNROLL):
            gbt[list_b[2, 2 * (i * UNROLL + u)]] += parts[u]
        return c

    lax.fori_loop(0, (list_b[3, 0] + UNROLL - 1) // UNROLL, backward, 0)

    def finish_own(i, c):
        own[pl.ds(i * TILE, TILE), :] = gbt[i].T
        return c

    lax.fori_loop(0, DST, finish_own, 0, unroll=4)
    bias_sum = jnp.sum(gb[...], axis=0, keepdims=True)
    row = iota((16, TILE), 0)
    bias_rows = jnp.where(
        row == 0, bias_sum[:, :TILE], jnp.where(row == 1, bias_sum[:, TILE:], 0.0)
    ).astype(BF)
    for i in range(WIDE // QUADS):
        at = pl.ds(i * QUADS, QUADS)
        bound[at] = gbt[DST + i].T.astype(BF).reshape(QUADS, SLOT, TILE)
        hubs[at] = gbt[DST + WIDE // QUADS + i].T.astype(BF).reshape(QUADS, SLOT, TILE)
    for p in range(WIDE):
        part = wg[pl.ds(8 * p, 8), :]
        sums[p, pl.ds(0, 16), :] = jnp.concatenate(
            [part[:, :TILE], part[:, TILE:]], axis=0
        ).astype(BF)
        sums[p, pl.ds(16, 16), :] = bias_rows
    out_hidden.wait()


def layer(list_f, list_b, wbuf, buf, cotb, w2, bias):
    vmem = pl.BlockSpec(memory_space=pltpu.VMEM)
    hbm = pl.BlockSpec(memory_space=pltpu.HBM)
    return pl.pallas_call(
        layer_kernel,
        out_shape=(
            jax.ShapeDtypeStruct((DST * TILE, 2 * TILE), BF),
            pltpu.VMEM((DST * TILE, TILE), F32),
            pltpu.VMEM((WIDE, SLOT, TILE), BF),
            pltpu.VMEM((WIDE, SLOT, TILE), BF),
            pltpu.VMEM((WIDE, SLOT, TILE), BF),
        ),
        in_specs=[hbm, hbm, vmem, vmem, vmem, vmem, vmem],
        out_specs=(hbm, vmem, vmem, vmem, vmem),
        scratch_shapes=[
            pltpu.SMEM((4, SLOTS), I32),
            pltpu.SMEM((4, SLOTS), I32),
            pltpu.VMEM((DST * TILE, 2 * TILE), BF),
            pltpu.VMEM((DST + 1, TILE, TILE), F32),
            pltpu.VMEM((DST + 1, TILE, TILE), BF),
            pltpu.VMEM((SRC + 1, TILE, TILE), F32),
            pltpu.VMEM((2 * TILE, 2 * TILE), F32),
            pltpu.VMEM((8, 2 * TILE), F32),
            pltpu.SemaphoreType.DMA((3,)),
        ],
        compiler_params=pltpu.CompilerParams(vmem_limit_bytes=30 * 2**20),
    )(
        in_hbm(list_f), in_hbm(list_b),
        in_vmem(wbuf), in_vmem(buf), in_vmem(cotb), in_vmem(w2), in_vmem(bias),
    )


def reduce_kernel(
    hub_rows, send_rows, own, bound, sums, hubs, acc, whole, total_bias,
    hub_at, send_at, hot, back, sum_in, hub_in, sum_out, sum_near, hub_out, hub_near, part,
    s_back, r_back, s_sum, r_sum, s_hub, r_hub, s_part, r_part,
    s_sum_near, r_sum_near, s_hub_near, r_hub_near, s_in,
):
    w = lax.axis_index("wide")
    n = lax.axis_index("narrow")
    loads = [
        pltpu.make_async_copy(hub_rows, hub_at, s_in.at[0]),
        pltpu.make_async_copy(send_rows, send_at, s_in.at[1]),
    ]
    for c in loads:
        c.start()
    barrier = greet_all(w, n)
    pl.semaphore_wait(barrier, WIDE - 1 + NARROW - 1)

    def wide_copy(o, src, dst, send, recv):
        return pltpu.make_async_remote_copy(
            src_ref=src,
            dst_ref=dst,
            send_sem=send.at[o],
            recv_sem=recv.at[o],
            device_id=(lax.rem(w + o, WIDE), n),
            device_id_type=MESH,
        )

    def near_copy(k, src, dst, send, recv):
        return pltpu.make_async_remote_copy(
            src_ref=src,
            dst_ref=dst,
            send_sem=send.at[k],
            recv_sem=recv.at[k],
            device_id=(w, lax.rem(n + k, NARROW)),
            device_id_type=MESH,
        )

    def sum_copy(o, slot):
        return wide_copy(o, sums.at[lax.rem(w + o, WIDE)], sum_in.at[slot], s_sum, r_sum)

    def hub_copy(o, slot):
        return wide_copy(o, hubs.at[lax.rem(w + o, WIDE)], hub_in.at[slot], s_hub, r_hub)

    def back_copy(o, slot):
        return wide_copy(o, bound.at[lax.rem(w + o, WIDE)], back.at[slot], s_back, r_back)

    def part_copy(o, slot):
        return wide_copy(o, part, whole.at[slot], s_part, r_part)

    def sum_near_copy(k, slot):
        return near_copy(k, sum_out, sum_near.at[slot], s_sum_near, r_sum_near)

    def hub_near_copy(k, slot):
        peer = lax.rem(n + k, NARROW)
        return near_copy(k, hub_out.at[peer], hub_near.at[slot], s_hub_near, r_hub_near)

    def send(copy):
        def one(o, c):
            copy(o, w).start()
            return c

        lax.fori_loop(1, WIDE, one, 0)

    def arrive(copy):
        def one(o, c):
            copy(o, lax.rem(w + WIDE - o, WIDE)).wait_recv()
            return c

        lax.fori_loop(1, WIDE, one, 0)

    def near_arrive(copy):
        for k in range(1, NARROW):
            copy(k, lax.rem(n + NARROW - k, NARROW)).wait_recv()

    send(sum_copy)
    send(hub_copy)
    send(back_copy)
    sum_in[w] = sums[w]
    hub_in[w] = hubs[w]
    back[w] = bound[w]

    for c in loads:
        c.wait()
    lane = iota((1, TILE), 1)
    hub_lane = jnp.full((1, TILE), -1, I32)
    for j in range(HUB):
        hub_lane = jnp.where((lane == j) | (lane == j + HUB), hub_at[j], hub_lane)
    where = jnp.concatenate(
        [send_at[pl.ds(p, 1), :] for p in range(WIDE)] + [hub_lane], axis=1
    )
    step, span = 512, WIDE * SLOT + TILE

    def mark(i, c):
        hit = iota((step, span), 0) + i * step == where
        hot[pl.ds(i * step, step), :] = jnp.where(hit, 1.0, 0.0).astype(BF)
        return c

    lax.fori_loop(0, DST * TILE // step, mark, 0)

    def add_up(ref, rows):
        def one(q, total):
            return total + ref[q].astype(F32)

        return lax.fori_loop(0, WIDE, one, jnp.zeros((rows, TILE), F32))

    arrive(sum_copy)
    sum_out[...] = add_up(sum_in, SLOT)[:24]
    sum_near[n] = sum_out[...]
    for k in range(1, NARROW):
        sum_near_copy(k, n).start()
    arrive(hub_copy)
    hub_sum = add_up(hub_in, SLOT)
    for k in range(NARROW):
        hub_out[k] = hub_sum[HUB * k : HUB * (k + 1)]
    hub_near[n] = hub_out[n]
    for k in range(1, NARROW):
        hub_near_copy(k, n).start()
    near_arrive(sum_near_copy)
    near = sum_near[0] + sum_near[1] + sum_near[2] + sum_near[3]
    part[...] = near[0:16].astype(BF)
    whole[w] = near[0:16].astype(BF)
    send(part_copy)
    total_bias[...] = near[16:24]

    near_arrive(hub_near_copy)
    mine = hub_near[0] + hub_near[1] + hub_near[2] + hub_near[3]
    high = mine.astype(BF)
    low = (mine - high.astype(F32)).astype(BF)
    arrive(back_copy)
    values = jnp.concatenate(
        [
            back[...].reshape(WIDE * SLOT, TILE),
            jnp.concatenate([high, low], axis=0),
            jnp.zeros((TILE - 2 * HUB, TILE), BF),
        ],
        axis=0,
    )

    def scatter(i, c):
        at = pl.ds(i * step, step)
        acc[at, :] = own[at, :] + mm(hot[at, :], values)
        return c

    lax.fori_loop(0, DST * TILE // step, scatter, 0)
    arrive(part_copy)

    def sent(o, c):
        sum_copy(o, w).wait_send()
        hub_copy(o, w).wait_send()
        back_copy(o, w).wait_send()
        part_copy(o, w).wait_send()
        return c

    lax.fori_loop(1, WIDE, sent, 0)
    for k in range(1, NARROW):
        sum_near_copy(k, n).wait_send()
        hub_near_copy(k, n).wait_send()


def reduce(hub_rows, send_rows, own, bound, sums, hubs):
    vmem = pl.BlockSpec(memory_space=pltpu.VMEM)
    hbm = pl.BlockSpec(memory_space=pltpu.HBM)
    dma = pltpu.SemaphoreType.DMA
    return pl.pallas_call(
        reduce_kernel,
        out_shape=(
            pltpu.VMEM((DST * TILE, TILE), F32),
            pltpu.VMEM((WIDE, 16, TILE), BF),
            pltpu.VMEM((8, TILE), F32),
        ),
        in_specs=[hbm, hbm, vmem, vmem, vmem, vmem],
        out_specs=(vmem, vmem, vmem),
        scratch_shapes=[
            pltpu.SMEM((HUB,), I32),
            pltpu.VMEM((WIDE, SLOT), I32),
            pltpu.VMEM((DST * TILE, WIDE * SLOT + TILE), BF),
            pltpu.VMEM((WIDE, SLOT, TILE), BF),
            pltpu.VMEM((WIDE, SLOT, TILE), BF),
            pltpu.VMEM((WIDE, SLOT, TILE), BF),
            pltpu.VMEM((24, TILE), F32),
            pltpu.VMEM((NARROW, 24, TILE), F32),
            pltpu.VMEM((NARROW, HUB, TILE), F32),
            pltpu.VMEM((NARROW, HUB, TILE), F32),
            pltpu.VMEM((16, TILE), BF),
            dma((WIDE,)), dma((WIDE,)), dma((WIDE,)), dma((WIDE,)),
            dma((WIDE,)), dma((WIDE,)), dma((WIDE,)), dma((WIDE,)),
            dma((NARROW,)), dma((NARROW,)), dma((NARROW,)), dma((NARROW,)), dma((2,)),
        ],
        compiler_params=pltpu.CompilerParams(
            collective_id=1, has_side_effects=True, vmem_limit_bytes=30 * 2**20
        ),
    )(
        in_hbm(hub_rows), in_hbm(send_rows),
        in_vmem(own), in_vmem(bound), in_vmem(sums), in_vmem(hubs),
    )


def finish_kernel(acc, whole, total_bias, gfeat, g_self, g_neigh, g_bias, weights, bias, sem):
    store = pltpu.make_async_copy(acc, gfeat, sem.at[0])
    store.start()
    for p in range(WIDE):
        got = whole[p].astype(F32)
        weights[pl.ds(8 * p, 8), :] = jnp.concatenate([got[:8], got[8:]], axis=1)
    bias[...] = jnp.concatenate([total_bias[pl.ds(0, 1), :], total_bias[pl.ds(1, 1), :]], axis=1)
    outs = [
        pltpu.make_async_copy(weights.at[pl.ds(0, TILE)], g_self, sem.at[1]),
        pltpu.make_async_copy(weights.at[pl.ds(TILE, TILE)], g_neigh, sem.at[2]),
        pltpu.make_async_copy(bias, g_bias, sem.at[3]),
    ]
    for c in outs:
        c.start()
    store.wait()
    for c in outs:
        c.wait()


def finish(acc, whole, total_bias):
    vmem = pl.BlockSpec(memory_space=pltpu.VMEM)
    hbm = pl.BlockSpec(memory_space=pltpu.HBM)
    return pl.pallas_call(
        finish_kernel,
        out_shape=(
            jax.ShapeDtypeStruct((DST * TILE, TILE), F32),
            jax.ShapeDtypeStruct((TILE, 2 * TILE), F32),
            jax.ShapeDtypeStruct((TILE, 2 * TILE), F32),
            jax.ShapeDtypeStruct((1, 2 * TILE), F32),
        ),
        in_specs=[vmem, vmem, vmem],
        out_specs=(hbm, hbm, hbm, hbm),
        scratch_shapes=[
            pltpu.VMEM((2 * TILE, 2 * TILE), F32),
            pltpu.VMEM((1, 2 * TILE), F32),
            pltpu.SemaphoreType.DMA((4,)),
        ],
    )(in_vmem(acc), in_vmem(whole), in_vmem(total_bias))


def on_device(
    features, cotangent, w_self, w_neigh, bias, tile_weights, tile_src, tile_dst, tile_live,
    send_rows, hub_rows,
):
    lanes = (TILES // TILE, TILE)
    wbuf, buf, cotb, w2, b2, list_f, list_b = fetch(
        features.reshape(DST * QUADS, SLOT, TILE), cotangent, w_self, w_neigh,
        bias.reshape(1, 2 * TILE), tile_weights,
        tile_src.reshape(lanes), tile_dst.reshape(lanes), tile_live.reshape(lanes),
        send_rows, hub_rows,
    )
    hidden, own, bound, sums, hubs = layer(list_f, list_b, wbuf, buf, cotb, w2, b2)
    acc, whole, total_bias = reduce(hub_rows, send_rows, own, bound, sums, hubs)
    grad_features, grad_self, grad_neigh, grad_bias = finish(acc, whole, total_bias)
    return (hidden, grad_features, grad_self, grad_neigh, grad_bias.reshape(2 * TILE))


def solution(mesh):
    both = ("wide", "narrow")
    placed = (
        P(both, None), P(both, None), P(), P(), P(), P(both, None, None),
        P(both), P(both), P(both), P(both, None), P(both),
    )
    return jax.shard_map(
        on_device,
        mesh=mesh,
        in_specs=placed,
        out_specs=(P(both, None), P(both, None), P(), P(), P()),
        check_vma=False,
    )
```

time: 90.5 us -> 65.8 us (0.73)
  local copies, waits for them, and re-layouts: 14.2 us -> 0 us
  Pallas kernels: 73.1 us -> 64.9 us
  other arithmetic: 1.54 us -> 0 us
    unnamed x30 -> x0, local copies, waits for them, and re-layouts: 13.4 us -> none
    pallas_call x1, Pallas kernels: 27.4 us -> 18.8 us  [layer(): pl.pallas_call(layer_kernel, out_shape=(jax.ShapeDtypeStruct((DST * TILE,...]
    concatenate x1 -> x0, other arithmetic: 1.54 us -> none  [on_device(): w2 = jnp.concatenate([w_self, w_neigh], axis=0)]
    pallas_call x2 -> x3, Pallas kernels: 45.6 us -> 46 us  [the longest x1 25.2 us: reduce(): pl.pallas_call(reduce_kernel, out_shape=(pltpu.VMEM((DST * TILE, TILE), F...]
where the time goes in v2:
time: 65.8 us; the launch traced here: 65.5 us
  Pallas kernels  64.9 us (99%)
  between operations  0.66 us (1%)
    pallas_call x1, Pallas kernels, reduce(): pl.pallas_call(reduce_kernel, out_shape=(pltpu.VMEM((DST * TILE, TILE), F...  25.2 us
    pallas_call x1, Pallas kernels, fetch(): pl.pallas_call(fetch_kernel, out_shape=(pltpu.VMEM((TILES, TILE, TILE), B...  19.4 us
    pallas_call x1, Pallas kernels, layer(): pl.pallas_call(layer_kernel, out_shape=(jax.ShapeDtypeStruct((DST * TILE,...  18.8 us
    pallas_call x1, Pallas kernels, finish(): pl.pallas_call(finish_kernel, out_shape=(jax.ShapeDtypeStruct((DST * TILE...  1.43 us

profile of v2, /device:TPU:1, one launch (start us, length us, event | category | flops | bytes accessed | tf_op | source)
XLA Modules:
  0.0 65.5 jit_solution(2316745276844597108)
XLA Ops:
  0.6 19.4 %shard_map.146 = (bf16[512,128,128]{2,1,0:T(8,128)(2,1)S(1)}, bf16[196,32,128]{2,1,0:T(8,128)(2,1)S(1)}, bf16[4096,256]{1,0:T(8,128)(2,1)S(1)}, bf16[256,256]{1,...) custom-call(bf16[128,32,128]{2,1,0:T(8,128)(2,1)} %bitcast.6, ...), custom_call_target="tpu_custom_call" | custom-call | tf_op jit(solution)/shard_map/pallas_call | solution.py:246
  20.0 18.8 %shard_map.147 = (bf16[4096,256]{1,0:T(8,128)(2,1)}, f32[4096,128]{1,0:T(8,128)S(1)}, bf16[32,32,128]{2,1,0:T(8,128)(2,1)S(1)}, bf16[32,32,128]{2,1,0:T(8,128)(2,1)S(1)}, bf16[32,32,128]{2,1,0:T(8,128)(2,1)S(1)}) custom-call(s32[4,640]{1,0:T(4,128)} %get-tuple-element.24.lists_f, s32[4,640]{1,0:T(4,128)} %get-tuple-element.25.lists_b, ...), custom_call_target="tpu_custom_call" | custom-call | tf_op jit(solution)/shard_map/pallas_call | solution.py:391
  38.9 25.2 %shard_map.148 = (f32[4096,128]{1,0:T(8,128)S(1)}, bf16[32,16,128]{2,1,0:T(8,128)(2,1)S(1)}, f32[8,128]{1,0:T(8,128)S(1)}) custom-call(s32[8]{0:T(128)} %hub_rows.3, s32[32,32]{1,0:T(8,128)} %send_rows.3, f32[4096,128]{1,0:T(8,128)S(1)} %get-tuple-element.32.own, bf16[32,32,128]{2,1,0:T(8,128)(2,1)S(1)} %get-tuple-element.33.bound, ...), custom_call_target="tpu_custom_call" | custom-call | tf_op jit(solution)/shard_map/pallas_call | solution.py:583
  64.1 1.4 %shard_map.149 = (f32[4096,128]{1,0:T(8,128)}, f32[128,256]{1,0:T(8,128)}, f32[128,256]{1,0:T(8,128)}, f32[1,256]{1,0:T(1,128)}) custom-call(f32[4096,128]{1,0:T(8,128)S(1)} %get-tuple-element.36.acc, bf16[32,16,128]{2,1,0:T(8,128)(2,1)S(1)} %get-tuple-element.37.whole, f32[8,128]{1,0:T(8,128)S(1)} %get-tuple-element.38.total_bias), custom_call_target="tpu_custom_call" | custom-call | tf_op jit(solution)/shard_map/pallas_call | solution.py:639

commit v3 on v2

--- a/solution.py
+++ b/solution.py
@@ -15,8 +15,11 @@
 TILES = 512
 SLOTS = 640
 UNROLL = 16
+PAIRS = 288
+COUNT = 64
 ROWS = 1024
 CHUNKS = 8
+VMEM_LIMIT = 32 * 2**20
 SLOT = 32
 QUADS = TILE // SLOT
 HUB = 8
@@ -62,17 +65,19 @@
     for r, v in enumerate(rows):
         values = jnp.where(row == r, v, values)
     got = nt(values.astype(F32).astype(BF), at).astype(I32)
-    pairs = (total * 0.5).astype(I32)
-    out = jnp.concatenate(
+    last = jnp.where(even > 0, (start + even) * 0.5 - 1.0, float(PAIRS))
+    across = iota((groups, TILE), 0) == iota((groups, TILE), 1)
+    last = jnp.sum(jnp.where(across, last, 0.0), axis=0, keepdims=True)
+    info = jnp.where(iota((1, TILE), 1) < groups, last, total * 0.5).astype(I32)
+    return jnp.concatenate(
         [
             got[0:1] * 16 + got[1:2],
             got[2:3] + zero,
             got[3:4] + keys,
-            jnp.broadcast_to(pairs, (1, SLOTS)),
+            jnp.concatenate([info, jnp.zeros((1, SLOTS - TILE), I32)], axis=1),
         ],
         axis=0,
     )
-    return out
 
 
 def greet_all(w, n):
@@ -271,45 +276,30 @@
             dma((NARROW,)), dma((NARROW,)), dma((2,)), dma((6,)), dma((4 + CHUNKS,)), dma((2,)),
         ],
         compiler_params=pltpu.CompilerParams(
-            collective_id=0, has_side_effects=True, vmem_limit_bytes=30 * 2**20
+            collective_id=0, has_side_effects=True, vmem_limit_bytes=VMEM_LIMIT
         ),
     )(
         *map(in_hbm, (feat, cot, w_self, w_neigh, bias, tiles, src, dst, live, send_rows, hub_rows))
     )
 
 
-def layer_kernel(
-    lists_f, lists_b, wbuf, buf, cotb, w2, bias, hidden, own, bound, sums, hubs,
-    list_f, list_b, hidb, agg, gt, gbt, wg, gb, sem,
+def forward_kernel(
+    lists_f, wbuf, buf, cotb, w2, bias, hidden, aggregate, grad_pre, list_f, agg, hid, sem, s_hid
 ):
-    loads = [
-        pltpu.make_async_copy(lists_f, list_f, sem.at[0]),
-        pltpu.make_async_copy(lists_b, list_b, sem.at[1]),
-    ]
-    for c in loads:
-        c.start()
+    load = pltpu.make_async_copy(lists_f, list_f, sem.at[0])
+    load.start()
 
     def clear(i, c):
         agg[i] = jnp.zeros((TILE, TILE), F32)
         return c
 
     lax.fori_loop(0, DST + 1, clear, 0)
-
-    def clear_back(i, c):
-        gbt[DST + i] = jnp.zeros((TILE, TILE), F32)
-        return c
-
-    lax.fori_loop(0, SRC - DST + 1, clear_back, 0)
-    gt[DST] = jnp.zeros((TILE, TILE), BF)
-    gb[...] = jnp.zeros_like(gb)
-    wg[...] = jnp.zeros_like(wg)
-    for c in loads:
-        c.wait()
+    load.wait()
 
     def rows_of(s):
         return buf[pl.ds(s * QUADS, QUADS)].reshape(TILE, TILE)
 
-    def forward(i, c):
+    def step(i, c):
         parts = []
         for u in range(UNROLL):
             k = 2 * (i * UNROLL + u)
@@ -322,116 +312,104 @@
             agg[list_f[2, 2 * (i * UNROLL + u)]] += parts[u]
         return c
 
-    lax.fori_loop(0, (list_f[3, 0] + UNROLL - 1) // UNROLL, forward, 0)
+    lax.fori_loop(0, (list_f[3, COUNT] + UNROLL - 1) // UNROLL, step, 0)
     blocks = ROWS // TILE
 
-    def dense(i, c):
+    def out_hidden(i):
         rows = pl.ds(i * ROWS, ROWS)
+        return pltpu.make_async_copy(hid.at[rows, :], hidden.at[rows, :], s_hid.at[i])
+
+    def activate(i, c):
+        rows, at = pl.ds(i * ROWS, ROWS), pl.ds(i * blocks, blocks)
         f = buf[pl.ds(i * blocks * QUADS, blocks * QUADS)].reshape(ROWS, TILE)
-        a = agg[pl.ds(i * blocks, blocks)].reshape(ROWS, TILE).astype(BF)
-        x = jnp.concatenate([f, a], axis=1)
-        pre = mm(x, w2[...]) + bias[...]
+        a = agg[at].astype(BF)
+        aggregate[at] = a
+        pre = mm(jnp.concatenate([f, a.reshape(ROWS, TILE)], axis=1), w2[...]) + bias[...]
         square = pre * pre
         t = jnp.tanh(pre * (GELU_A + (GELU_A * GELU_B) * square))
         half = 0.5 + 0.5 * t
-        hidb[rows, :] = (pre * half).astype(BF)
+        hid[rows, :] = (pre * half).astype(BF)
+        out_hidden(i).start()
         slope = half + pre * (0.5 - 0.5 * t * t) * (GELU_A + (3 * GELU_A * GELU_B) * square)
-        gp = (cotb[rows, :].astype(F32) * slope).astype(BF)
-        wg[...] += tn(x, gp)
-        gb[...] += jnp.sum(gp.astype(F32).reshape(ROWS // 8, 8, 2 * TILE), axis=0)
-        g2 = nt(w2[...], gp)
-        for j in range(blocks):
-            gbt[i * blocks + j] = g2[:TILE, j * TILE : (j + 1) * TILE]
-            gt[i * blocks + j] = g2[TILE:, j * TILE : (j + 1) * TILE].astype(BF)
-        return c
-
-    lax.fori_loop(0, DST // blocks, dense, 0)
-    out_hidden = pltpu.make_async_copy(hidb, hidden, sem.at[2])
-    out_hidden.start()
-
-    def backward(i, c):
-        parts = []
-        for u in range(UNROLL):
-            k = 2 * (i * UNROLL + u)
-            left = jnp.concatenate([gt[list_b[1, k]], gt[list_b[1, k + 1]]], axis=1)
-            right = jnp.concatenate([wbuf[list_b[0, k]], wbuf[list_b[0, k + 1]]], axis=0)
-            parts.append(mm(left, right))
-        for u in range(UNROLL):
-            gbt[list_b[2, 2 * (i * UNROLL + u)]] += parts[u]
-        return c
-
-    lax.fori_loop(0, (list_b[3, 0] + UNROLL - 1) // UNROLL, backward, 0)
-
-    def finish_own(i, c):
-        own[pl.ds(i * TILE, TILE), :] = gbt[i].T
-        return c
-
-    lax.fori_loop(0, DST, finish_own, 0, unroll=4)
-    bias_sum = jnp.sum(gb[...], axis=0, keepdims=True)
-    row = iota((16, TILE), 0)
-    bias_rows = jnp.where(
-        row == 0, bias_sum[:, :TILE], jnp.where(row == 1, bias_sum[:, TILE:], 0.0)
-    ).astype(BF)
-    for i in range(WIDE // QUADS):
-        at = pl.ds(i * QUADS, QUADS)
-        bound[at] = gbt[DST + i].T.astype(BF).reshape(QUADS, SLOT, TILE)
-        hubs[at] = gbt[DST + WIDE // QUADS + i].T.astype(BF).reshape(QUADS, SLOT, TILE)
-    for p in range(WIDE):
-        part = wg[pl.ds(8 * p, 8), :]
-        sums[p, pl.ds(0, 16), :] = jnp.concatenate(
-            [part[:, :TILE], part[:, TILE:]], axis=0
-        ).astype(BF)
-        sums[p, pl.ds(16, 16), :] = bias_rows
-    out_hidden.wait()
-
-
-def layer(list_f, list_b, wbuf, buf, cotb, w2, bias):
+        grad_pre[rows, :] = (cotb[rows, :].astype(F32) * slope).astype(BF)
+        return c
+
+    lax.fori_loop(0, DST // blocks, activate, 0)
+    for i in range(DST // blocks):
+        out_hidden(i).wait()
+
+
+def forward(list_f, wbuf, buf, cotb, w2, bias):
     vmem = pl.BlockSpec(memory_space=pltpu.VMEM)
     hbm = pl.BlockSpec(memory_space=pltpu.HBM)
     return pl.pallas_call(
-        layer_kernel,
+        forward_kernel,
         out_shape=(
             jax.ShapeDtypeStruct((DST * TILE, 2 * TILE), BF),
-            pltpu.VMEM((DST * TILE, TILE), F32),
-            pltpu.VMEM((WIDE, SLOT, TILE), BF),
-            pltpu.VMEM((WIDE, SLOT, TILE), BF),
-            pltpu.VMEM((WIDE, SLOT, TILE), BF),
+            pltpu.VMEM((DST, TILE, TILE), BF),
+            pltpu.VMEM((DST * TILE, 2 * TILE), BF),
         ),
-        in_specs=[hbm, hbm, vmem, vmem, vmem, vmem, vmem],
-        out_specs=(hbm, vmem, vmem, vmem, vmem),
+        in_specs=[hbm] + [vmem] * 5,
+        out_specs=(hbm, vmem, vmem),
         scratch_shapes=[
             pltpu.SMEM((4, SLOTS), I32),
-            pltpu.SMEM((4, SLOTS), I32),
+            pltpu.VMEM((DST + 1, TILE, TILE), F32),
             pltpu.VMEM((DST * TILE, 2 * TILE), BF),
-            pltpu.VMEM((DST + 1, TILE, TILE), F32),
-            pltpu.VMEM((DST + 1, TILE, TILE), BF),
-            pltpu.VMEM((SRC + 1, TILE, TILE), F32),
-            pltpu.VMEM((2 * TILE, 2 * TILE), F32),
-            pltpu.VMEM((8, 2 * TILE), F32),
-            pltpu.SemaphoreType.DMA((3,)),
+            pltpu.SemaphoreType.DMA((1,)),
+            pltpu.SemaphoreType.DMA((DST * TILE // ROWS,)),
         ],
-        compiler_params=pltpu.CompilerParams(vmem_limit_bytes=30 * 2**20),
-    )(
-        in_hbm(list_f), in_hbm(list_b),
-        in_vmem(wbuf), in_vmem(buf), in_vmem(cotb), in_vmem(w2), in_vmem(bias),
-    )
-
-
-def reduce_kernel(
-    hub_rows, send_rows, own, bound, sums, hubs, acc, whole, total_bias,
-    hub_at, send_at, hot, back, sum_in, hub_in, sum_out, sum_near, hub_out, hub_near, part,
+        compiler_params=pltpu.CompilerParams(vmem_limit_bytes=VMEM_LIMIT),
+    )(in_hbm(list_f), *map(in_vmem, (wbuf, buf, cotb, w2, bias)))
+
+
+def backward_kernel(
+    lists_b, hub_rows, send_rows, wbuf, buf, w2, aggregate, grad_pre, acc, whole, total_bias,
+    list_b, hub_at, send_at, slots, gt, wg, gb, sums, bound, hubs,
+    back, sum_in, hub_in, sum_out, sum_near, hub_out, hub_near, part,
     s_back, r_back, s_sum, r_sum, s_hub, r_hub, s_part, r_part,
     s_sum_near, r_sum_near, s_hub_near, r_hub_near, s_in,
 ):
     w = lax.axis_index("wide")
     n = lax.axis_index("narrow")
     loads = [
-        pltpu.make_async_copy(hub_rows, hub_at, s_in.at[0]),
-        pltpu.make_async_copy(send_rows, send_at, s_in.at[1]),
+        pltpu.make_async_copy(lists_b, list_b, s_in.at[0]),
+        pltpu.make_async_copy(hub_rows, hub_at, s_in.at[1]),
+        pltpu.make_async_copy(send_rows, send_at, s_in.at[2]),
     ]
     for c in loads:
         c.start()
     barrier = greet_all(w, n)
+    gb[...] = jnp.zeros_like(gb)
+    wg[...] = jnp.zeros_like(wg)
+    gt[DST] = jnp.zeros((TILE, TILE), BF)
+    slots[PAIRS] = jnp.zeros((TILE, TILE), F32)
+    blocks = ROWS // TILE
+
+    def dense(i, c):
+        rows = pl.ds(i * ROWS, ROWS)
+        f = buf[pl.ds(i * blocks * QUADS, blocks * QUADS)].reshape(ROWS, TILE)
+        x = jnp.concatenate([f, aggregate[pl.ds(i * blocks, blocks)].reshape(ROWS, TILE)], axis=1)
+        gp = grad_pre[rows, :]
+        wg[...] += tn(x, gp)
+        gb[...] += jnp.sum(gp.astype(F32).reshape(ROWS // 8, 8, 2 * TILE), axis=0)
+        acc[rows, :] = nt(gp, w2[pl.ds(0, TILE), :])
+        g = nt(w2[pl.ds(TILE, TILE), :], gp).astype(BF)
+        for j in range(blocks):
+            gt[i * blocks + j] = g[:, j * TILE : (j + 1) * TILE]
+        return c
+
+    lax.fori_loop(0, DST // blocks, dense, 0)
+    bias_sum = jnp.sum(gb[...], axis=0, keepdims=True)
+    row = iota((16, TILE), 0)
+    bias_rows = jnp.where(
+        row == 0, bias_sum[:, :TILE], jnp.where(row == 1, bias_sum[:, TILE:], 0.0)
+    ).astype(BF)
+    for p in range(WIDE):
+        rows = wg[pl.ds(8 * p, 8), :]
+        sums[p, pl.ds(0, 16), :] = jnp.concatenate(
+            [rows[:, :TILE], rows[:, TILE:]], axis=0
+        ).astype(BF)
+        sums[p, pl.ds(16, 16), :] = bias_rows
     pl.semaphore_wait(barrier, WIDE - 1 + NARROW - 1)
 
     def wide_copy(o, src, dst, send, recv):
@@ -491,42 +469,71 @@
         for k in range(1, NARROW):
             copy(k, lax.rem(n + NARROW - k, NARROW)).wait_recv()
 
-    send(sum_copy)
-    send(hub_copy)
-    send(back_copy)
-    sum_in[w] = sums[w]
-    hub_in[w] = hubs[w]
-    back[w] = bound[w]
-
-    for c in loads:
-        c.wait()
-    lane = iota((1, TILE), 1)
-    hub_lane = jnp.full((1, TILE), -1, I32)
-    for j in range(HUB):
-        hub_lane = jnp.where((lane == j) | (lane == j + HUB), hub_at[j], hub_lane)
-    where = jnp.concatenate(
-        [send_at[pl.ds(p, 1), :] for p in range(WIDE)] + [hub_lane], axis=1
-    )
-    step, span = 512, WIDE * SLOT + TILE
-
-    def mark(i, c):
-        hit = iota((step, span), 0) + i * step == where
-        hot[pl.ds(i * step, step), :] = jnp.where(hit, 1.0, 0.0).astype(BF)
-        return c
-
-    lax.fori_loop(0, DST * TILE // step, mark, 0)
-
     def add_up(ref, rows):
         def one(q, total):
             return total + ref[q].astype(F32)
 
         return lax.fori_loop(0, WIDE, one, jnp.zeros((rows, TILE), F32))
 
+    def walk(i, total):
+        parts = []
+        for u in range(UNROLL):
+            k = 2 * (i * UNROLL + u)
+            left = jnp.concatenate([gt[list_b[1, k]], gt[list_b[1, k + 1]]], axis=1)
+            right = jnp.concatenate([wbuf[list_b[0, k]], wbuf[list_b[0, k + 1]]], axis=0)
+            parts.append(mm(left, right))
+        for u in range(UNROLL):
+            k = i * UNROLL + u
+            same = list_b[2, 2 * k] == list_b[2, jnp.maximum(2 * k - 2, 0)]
+            total = total * same.astype(F32) + parts[u]
+            slots[k] = total
+        return total
+
+    send(sum_copy)
+    sum_in[w] = sums[w]
+    for c in loads:
+        c.wait()
+    steps = PAIRS // UNROLL
+    total = lax.fori_loop(0, steps // 2, walk, jnp.zeros((TILE, TILE), F32))
     arrive(sum_copy)
     sum_out[...] = add_up(sum_in, SLOT)[:24]
     sum_near[n] = sum_out[...]
     for k in range(1, NARROW):
         sum_near_copy(k, n).start()
+    lax.fori_loop(steps // 2, steps, walk, total)
+    near_arrive(sum_near_copy)
+    near = sum_near[0] + sum_near[1] + sum_near[2] + sum_near[3]
+    part[...] = near[0:16].astype(BF)
+    whole[w] = near[0:16].astype(BF)
+    total_bias[...] = near[16:24]
+
+    remote = WIDE // QUADS
+    for i in range(remote):
+        at = pl.ds(i * QUADS, QUADS)
+        total = slots[list_b[3, DST + remote + i]]
+        hubs[at] = total.T.astype(BF).reshape(QUADS, SLOT, TILE)
+    send(hub_copy)
+    for i in range(remote):
+        at = pl.ds(i * QUADS, QUADS)
+        total = slots[list_b[3, DST + i]]
+        bound[at] = total.T.astype(BF).reshape(QUADS, SLOT, TILE)
+    send(back_copy)
+    send(part_copy)
+    hub_in[w] = hubs[w]
+    back[w] = bound[w]
+
+    def add_own(i, c):
+        at = pl.ds(i * TILE, TILE)
+        acc[at, :] += slots[list_b[3, i]].T
+        return c
+
+    lax.fori_loop(0, DST, add_own, 0, unroll=4)
+    lane = iota((1, TILE), 1)
+    hub_lane = jnp.full((1, TILE), -1, I32)
+    for j in range(HUB):
+        hub_lane = jnp.where((lane == j) | (lane == j + HUB), hub_at[j], hub_lane)
+    row_lane = jnp.concatenate([send_at[pl.ds(p, 1), :] for p in range(WIDE)], axis=1)
+
     arrive(hub_copy)
     hub_sum = add_up(hub_in, SLOT)
     for k in range(NARROW):
@@ -534,33 +541,26 @@
     hub_near[n] = hub_out[n]
     for k in range(1, NARROW):
         hub_near_copy(k, n).start()
-    near_arrive(sum_near_copy)
-    near = sum_near[0] + sum_near[1] + sum_near[2] + sum_near[3]
-    part[...] = near[0:16].astype(BF)
-    whole[w] = near[0:16].astype(BF)
-    send(part_copy)
-    total_bias[...] = near[16:24]
-
+
+    def scatter(lanes, values):
+        step = 512
+
+        def one(i, c):
+            at = pl.ds(i * step, step)
+            hit = iota((step, lanes.shape[1]), 0) + i * step == lanes
+            acc[at, :] += mm(jnp.where(hit, 1.0, 0.0).astype(BF), values)
+            return c
+
+        lax.fori_loop(0, DST * TILE // step, one, 0)
+
+    arrive(back_copy)
+    scatter(row_lane, back[...].reshape(WIDE * SLOT, TILE))
     near_arrive(hub_near_copy)
     mine = hub_near[0] + hub_near[1] + hub_near[2] + hub_near[3]
     high = mine.astype(BF)
     low = (mine - high.astype(F32)).astype(BF)
-    arrive(back_copy)
-    values = jnp.concatenate(
-        [
-            back[...].reshape(WIDE * SLOT, TILE),
-            jnp.concatenate([high, low], axis=0),
-            jnp.zeros((TILE - 2 * HUB, TILE), BF),
-        ],
-        axis=0,
-    )
-
-    def scatter(i, c):
-        at = pl.ds(i * step, step)
-        acc[at, :] = own[at, :] + mm(hot[at, :], values)
-        return c
-
-    lax.fori_loop(0, DST * TILE // step, scatter, 0)
+    values = jnp.concatenate([high, low, jnp.zeros((TILE - 2 * HUB, TILE), BF)], axis=0)
+    scatter(hub_lane, values)
     arrive(part_copy)
 
     def sent(o, c):
@@ -576,23 +576,30 @@
         hub_near_copy(k, n).wait_send()
 
 
-def reduce(hub_rows, send_rows, own, bound, sums, hubs):
+def backward(list_b, hub_rows, send_rows, wbuf, buf, w2, aggregate, grad_pre):
     vmem = pl.BlockSpec(memory_space=pltpu.VMEM)
     hbm = pl.BlockSpec(memory_space=pltpu.HBM)
     dma = pltpu.SemaphoreType.DMA
     return pl.pallas_call(
-        reduce_kernel,
+        backward_kernel,
         out_shape=(
             pltpu.VMEM((DST * TILE, TILE), F32),
             pltpu.VMEM((WIDE, 16, TILE), BF),
             pltpu.VMEM((8, TILE), F32),
         ),
-        in_specs=[hbm, hbm, vmem, vmem, vmem, vmem],
-        out_specs=(vmem, vmem, vmem),
+        in_specs=[hbm] * 3 + [vmem] * 5,
+        out_specs=(vmem,) * 3,
         scratch_shapes=[
+            pltpu.SMEM((4, SLOTS), I32),
             pltpu.SMEM((HUB,), I32),
             pltpu.VMEM((WIDE, SLOT), I32),
-            pltpu.VMEM((DST * TILE, WIDE * SLOT + TILE), BF),
+            pltpu.VMEM((PAIRS + 1, TILE, TILE), F32),
+            pltpu.VMEM((DST + 1, TILE, TILE), BF),
+            pltpu.VMEM((2 * TILE, 2 * TILE), F32),
+            pltpu.VMEM((8, 2 * TILE), F32),
+            pltpu.VMEM((WIDE, SLOT, TILE), BF),
+            pltpu.VMEM((WIDE, SLOT, TILE), BF),
+            pltpu.VMEM((WIDE, SLOT, TILE), BF),
             pltpu.VMEM((WIDE, SLOT, TILE), BF),
             pltpu.VMEM((WIDE, SLOT, TILE), BF),
             pltpu.VMEM((WIDE, SLOT, TILE), BF),
@@ -603,14 +610,14 @@
             pltpu.VMEM((16, TILE), BF),
             dma((WIDE,)), dma((WIDE,)), dma((WIDE,)), dma((WIDE,)),
             dma((WIDE,)), dma((WIDE,)), dma((WIDE,)), dma((WIDE,)),
-            dma((NARROW,)), dma((NARROW,)), dma((NARROW,)), dma((NARROW,)), dma((2,)),
+            dma((NARROW,)), dma((NARROW,)), dma((NARROW,)), dma((NARROW,)), dma((3,)),
         ],
         compiler_params=pltpu.CompilerParams(
-            collective_id=1, has_side_effects=True, vmem_limit_bytes=30 * 2**20
+            collective_id=1, has_side_effects=True, vmem_limit_bytes=VMEM_LIMIT
         ),
     )(
-        in_hbm(hub_rows), in_hbm(send_rows),
-        in_vmem(own), in_vmem(bound), in_vmem(sums), in_vmem(hubs),
+        in_hbm(list_b), in_hbm(hub_rows), in_hbm(send_rows),
+        *map(in_vmem, (wbuf, buf, w2, aggregate, grad_pre)),
     )
 
 
@@ -628,8 +635,7 @@
     ]
     for c in outs:
         c.start()
-    store.wait()
-    for c in outs:
+    for c in [store] + outs:
         c.wait()
 
 
@@ -644,8 +650,8 @@
             jax.ShapeDtypeStruct((TILE, 2 * TILE), F32),
             jax.ShapeDtypeStruct((1, 2 * TILE), F32),
         ),
-        in_specs=[vmem, vmem, vmem],
-        out_specs=(hbm, hbm, hbm, hbm),
+        in_specs=[vmem] * 3,
+        out_specs=(hbm,) * 4,
         scratch_shapes=[
             pltpu.VMEM((2 * TILE, 2 * TILE), F32),
             pltpu.VMEM((1, 2 * TILE), F32),
@@ -665,8 +671,10 @@
         tile_src.reshape(lanes), tile_dst.reshape(lanes), tile_live.reshape(lanes),
         send_rows, hub_rows,
     )
-    hidden, own, bound, sums, hubs = layer(list_f, list_b, wbuf, buf, cotb, w2, b2)
-    acc, whole, total_bias = reduce(hub_rows, send_rows, own, bound, sums, hubs)
+    hidden, aggregate, grad_pre = forward(list_f, wbuf, buf, cotb, w2, b2)
+    acc, whole, total_bias = backward(
+        list_b, hub_rows, send_rows, wbuf, buf, w2, aggregate, grad_pre
+    )
     grad_features, grad_self, grad_neigh, grad_bias = finish(acc, whole, total_bias)
     return (hidden, grad_features, grad_self, grad_neigh, grad_bias.reshape(2 * TILE))
 

time: 65.8 us -> 65 us (0.988)
  Pallas kernels: 64.9 us -> 64.1 us
    pallas_call x2, Pallas kernels: 44 us -> 43.2 us  [the longest x1 32.3 us: backward(): pl.pallas_call(backward_kernel, out_shape=(pltpu.VMEM((DST * TILE, TILE),...]
where the time goes in v3:
time: 65 us; the launch traced here: 64.7 us
  Pallas kernels  64.1 us (99%)
  between operations  0.66 us (1%)
    pallas_call x1, Pallas kernels, backward(): pl.pallas_call(backward_kernel, out_shape=(pltpu.VMEM((DST * TILE, TILE),...  32.3 us
    pallas_call x1, Pallas kernels, fetch(): pl.pallas_call(fetch_kernel, out_shape=(pltpu.VMEM((TILES, TILE, TILE), B...  19.4 us
    pallas_call x1, Pallas kernels, forward(): pl.pallas_call(forward_kernel, out_shape=(jax.ShapeDtypeStruct((DST * TIL...  10.9 us
    pallas_call x1, Pallas kernels, finish(): pl.pallas_call(finish_kernel, out_shape=(jax.ShapeDtypeStruct((DST * TILE...  1.43 us

profile of v3, /device:TPU:1, one launch (start us, length us, event | category | flops | bytes accessed | tf_op | source)
XLA Modules:
  0.0 64.7 jit_solution(16334137261841250401)
XLA Ops:
  0.6 19.4 %shard_map.146 = (bf16[512,128,128]{2,1,0:T(8,128)(2,1)S(1)}, bf16[196,32,128]{2,1,0:T(8,128)(2,1)S(1)}, bf16[4096,256]{1,0:T(8,128)(2,1)S(1)}, bf16[256,256]{1,...) custom-call(bf16[128,32,128]{2,1,0:T(8,128)(2,1)} %bitcast.6, ...), custom_call_target="tpu_custom_call" | custom-call | tf_op jit(solution)/shard_map/pallas_call | solution.py:251
  20.0 10.9 %shard_map.147 = (bf16[4096,256]{1,0:T(8,128)(2,1)}, bf16[32,128,128]{2,1,0:T(8,128)(2,1)S(1)}, bf16[4096,256]{1,0:T(8,128)(2,1)S(1)}) custom-call(s32[4,640]{1,0:T(4,128)} %get-tuple-element.22.lists_f, bf16[512,128,128]{2,1,0:T(8,128)(2,1)S(1)} %get-tuple-element.23.wbuf, bf16[196,32,128]{2,1,0:T(8,128)(2,1)S(1)} %get-tuple-element.24.buf, ...), custom_call_target="tpu_custom_call" | custom-call | tf_op jit(solution)/shard_map/pallas_call | solution.py:345
  31.0 32.3 %shard_map.148 = (f32[4096,128]{1,0:T(8,128)S(1)}, bf16[32,16,128]{2,1,0:T(8,128)(2,1)S(1)}, f32[8,128]{1,0:T(8,128)S(1)}) custom-call(s32[4,640]{1,0:T(4,128)} %get-tuple-element.29.lists_b, s32[8]{0:T(128)} %hub_rows.3, s32[32,32]{1,0:T(8,128)} %send_rows.3, bf16[512,128,128]{2,1,0:T(8,128)(2,1)S(1)} %get-tuple-element.23.wbuf, ...), custom_call_target="tpu_custom_call" | custom-call | tf_op jit(solution)/shard_map/pallas_call | solution.py:583
  63.3 1.4 %shard_map.149 = (f32[4096,128]{1,0:T(8,128)}, f32[128,256]{1,0:T(8,128)}, f32[128,256]{1,0:T(8,128)}, f32[1,256]{1,0:T(1,128)}) custom-call(f32[4096,128]{1,0:T(8,128)S(1)} %get-tuple-element.32.acc, bf16[32,16,128]{2,1,0:T(8,128)(2,1)S(1)} %get-tuple-element.33.whole, f32[8,128]{1,0:T(8,128)S(1)} %get-tuple-element.34.total_bias), custom_call_target="tpu_custom_call" | custom-call | tf_op jit(solution)/shard_map/pallas_call | solution.py:645

commit v4 on v3

--- a/solution.py
+++ b/solution.py
@@ -14,8 +14,9 @@
 SRC = 48
 TILES = 512
 SLOTS = 640
-UNROLL = 16
-PAIRS = 288
+UNROLL = 24
+WALK = 34
+PAIRS = 272
 COUNT = 64
 ROWS = 1024
 CHUNKS = 8
@@ -98,8 +99,8 @@
 
 
 def fetch_kernel(
-    feat, cot, w_self, w_neigh, bias, tiles, src, dst, live, send_rows, hub_rows,
-    wbuf, buf, cotb, w2, b2, list_f, list_b,
+    feat, w_self, w_neigh, bias, tiles, src, dst, live, send_rows, hub_rows,
+    wbuf, buf, w2, b2, list_f, list_r, list_o,
     send_at, hub_at, keys, wide32, hubs, picked, msg, near, own, lists,
     s_row, r_row, s_hub, r_hub, s_near, r_near, s_own, s_in, s_big, s_list,
 ):
@@ -120,12 +121,11 @@
         pltpu.make_async_copy(w_self, w2.at[pl.ds(0, TILE)], s_big.at[0]),
         pltpu.make_async_copy(w_neigh, w2.at[pl.ds(TILE, TILE)], s_big.at[1]),
         pltpu.make_async_copy(bias, b2, s_big.at[2]),
-        pltpu.make_async_copy(cot, cotb, s_big.at[3]),
     ]
     per = TILES // CHUNKS
     big += [
         pltpu.make_async_copy(
-            tiles.at[pl.ds(i * per, per)], wbuf.at[pl.ds(i * per, per)], s_big.at[4 + i]
+            tiles.at[pl.ds(i * per, per)], wbuf.at[pl.ds(i * per, per)], s_big.at[3 + i]
         )
         for i in range(CHUNKS)
     ]
@@ -211,10 +211,11 @@
 
     s, d, l = flat(0), flat(1), flat(2)
     lists[0] = tile_list(d, s, l, DST, SRC)
-    lists[1] = tile_list(s, d, l, SRC, DST)
+    lists[1] = tile_list(s - DST, d, jnp.where(s >= DST, l, 0), SRC - DST, DST)
+    lists[2] = tile_list(s, d, jnp.where(s < DST, l, 0), DST, DST)
     out_lists = [
-        pltpu.make_async_copy(lists.at[0], list_f, s_list.at[0]),
-        pltpu.make_async_copy(lists.at[1], list_b, s_list.at[1]),
+        pltpu.make_async_copy(lists.at[i], out, s_list.at[i])
+        for i, out in enumerate((list_f, list_r, list_o))
     ]
     for c in out_lists:
         c.start()
@@ -244,7 +245,7 @@
     return pltpu.with_memory_space_constraint(x, pltpu.HBM)
 
 
-def fetch(feat, cot, w_self, w_neigh, bias, tiles, src, dst, live, send_rows, hub_rows):
+def fetch(*args):
     vmem = pl.BlockSpec(memory_space=pltpu.VMEM)
     hbm = pl.BlockSpec(memory_space=pltpu.HBM)
     dma = pltpu.SemaphoreType.DMA
@@ -253,14 +254,14 @@
         out_shape=(
             pltpu.VMEM((TILES, TILE, TILE), BF),
             pltpu.VMEM(((SRC + 1) * QUADS, SLOT, TILE), BF),
-            pltpu.VMEM((DST * TILE, 2 * TILE), BF),
             pltpu.VMEM((2 * TILE, 2 * TILE), BF),
             pltpu.VMEM((1, 2 * TILE), F32),
             pltpu.HBM((4, SLOTS), I32),
             pltpu.HBM((4, SLOTS), I32),
+            pltpu.HBM((4, SLOTS), I32),
         ),
-        in_specs=[hbm] * 11,
-        out_specs=(vmem, vmem, vmem, vmem, vmem, hbm, hbm),
+        in_specs=[hbm] * 10,
+        out_specs=(vmem,) * 4 + (hbm,) * 3,
         scratch_shapes=[
             pltpu.SMEM((WIDE, SLOT), I32),
             pltpu.SMEM((HUB,), I32),
@@ -271,30 +272,34 @@
             pltpu.VMEM((WIDE, SLOT, TILE), BF),
             pltpu.VMEM((NARROW, HUB, TILE), F32),
             pltpu.VMEM((NARROW * HUB, TILE), BF),
-            pltpu.VMEM((2, 4, SLOTS), I32),
+            pltpu.VMEM((3, 4, SLOTS), I32),
             dma((WIDE,)), dma((WIDE,)), dma((WIDE,)), dma((WIDE,)),
-            dma((NARROW,)), dma((NARROW,)), dma((2,)), dma((6,)), dma((4 + CHUNKS,)), dma((2,)),
+            dma((NARROW,)), dma((NARROW,)), dma((2,)), dma((6,)), dma((3 + CHUNKS,)), dma((3,)),
         ],
         compiler_params=pltpu.CompilerParams(
             collective_id=0, has_side_effects=True, vmem_limit_bytes=VMEM_LIMIT
         ),
-    )(
-        *map(in_hbm, (feat, cot, w_self, w_neigh, bias, tiles, src, dst, live, send_rows, hub_rows))
-    )
+    )(*map(in_hbm, args))
 
 
 def forward_kernel(
-    lists_f, wbuf, buf, cotb, w2, bias, hidden, aggregate, grad_pre, list_f, agg, hid, sem, s_hid
+    lists_f, lists_r, cot, wbuf, buf, w2, bias, hidden, grad_pre, gt, sums, bound, hub_out,
+    list_f, list_r, cotb, agg, hid, gbt, wg, gb, sem, s_hid,
 ):
-    load = pltpu.make_async_copy(lists_f, list_f, sem.at[0])
-    load.start()
+    loads = [
+        pltpu.make_async_copy(lists_f, list_f, sem.at[0]),
+        pltpu.make_async_copy(lists_r, list_r, sem.at[1]),
+        pltpu.make_async_copy(cot, cotb, sem.at[2]),
+    ]
+    for c in loads:
+        c.start()
 
     def clear(i, c):
         agg[i] = jnp.zeros((TILE, TILE), F32)
         return c
 
     lax.fori_loop(0, DST + 1, clear, 0)
-    load.wait()
+    loads[0].wait()
 
     def rows_of(s):
         return buf[pl.ds(s * QUADS, QUADS)].reshape(TILE, TILE)
@@ -313,6 +318,16 @@
         return c
 
     lax.fori_loop(0, (list_f[3, COUNT] + UNROLL - 1) // UNROLL, step, 0)
+    def clear_back(i, c):
+        gbt[i] = jnp.zeros((TILE, TILE), F32)
+        return c
+
+    lax.fori_loop(0, SRC - DST + 1, clear_back, 0)
+    gb[...] = jnp.zeros_like(gb)
+    wg[...] = jnp.zeros_like(wg)
+    gt[DST] = jnp.zeros((TILE, TILE), BF)
+    for c in loads[1:]:
+        c.wait()
     blocks = ROWS // TILE
 
     def out_hidden(i):
@@ -322,94 +337,112 @@
     def activate(i, c):
         rows, at = pl.ds(i * ROWS, ROWS), pl.ds(i * blocks, blocks)
         f = buf[pl.ds(i * blocks * QUADS, blocks * QUADS)].reshape(ROWS, TILE)
-        a = agg[at].astype(BF)
-        aggregate[at] = a
-        pre = mm(jnp.concatenate([f, a.reshape(ROWS, TILE)], axis=1), w2[...]) + bias[...]
+        a = agg[at].reshape(ROWS, TILE).astype(BF)
+        x = jnp.concatenate([f, a], axis=1)
+        pre = mm(x, w2[...]) + bias[...]
         square = pre * pre
         t = jnp.tanh(pre * (GELU_A + (GELU_A * GELU_B) * square))
         half = 0.5 + 0.5 * t
         hid[rows, :] = (pre * half).astype(BF)
         out_hidden(i).start()
         slope = half + pre * (0.5 - 0.5 * t * t) * (GELU_A + (3 * GELU_A * GELU_B) * square)
-        grad_pre[rows, :] = (cotb[rows, :].astype(F32) * slope).astype(BF)
+        gp = (cotb[rows, :].astype(F32) * slope).astype(BF)
+        grad_pre[rows, :] = gp
+        wg[...] += tn(x, gp)
+        gb[...] += jnp.sum(gp.astype(F32).reshape(ROWS // 8, 8, 2 * TILE), axis=0)
+        g = nt(w2[pl.ds(TILE, TILE), :], gp).astype(BF)
+        for j in range(blocks):
+            gt[i * blocks + j] = g[:, j * TILE : (j + 1) * TILE]
         return c
 
     lax.fori_loop(0, DST // blocks, activate, 0)
+
+    def step_back(i, c):
+        parts = []
+        for u in range(UNROLL):
+            k = 2 * (i * UNROLL + u)
+            left = jnp.concatenate([gt[list_r[1, k]], gt[list_r[1, k + 1]]], axis=1)
+            right = jnp.concatenate([wbuf[list_r[0, k]], wbuf[list_r[0, k + 1]]], axis=0)
+            parts.append(mm(left, right))
+        for u in range(UNROLL):
+            gbt[list_r[2, 2 * (i * UNROLL + u)]] += parts[u]
+        return c
+
+    lax.fori_loop(0, (list_r[3, COUNT] + UNROLL - 1) // UNROLL, step_back, 0)
+    bias_sum = jnp.sum(gb[...], axis=0, keepdims=True)
+    row = iota((16, TILE), 0)
+    bias_rows = jnp.where(
+        row == 0, bias_sum[:, :TILE], jnp.where(row == 1, bias_sum[:, TILE:], 0.0)
+    ).astype(BF)
+    for k in range(NARROW):
+        hub_out[k, pl.ds(WIDE * HUB, 16), :] = bias_rows
+    for p in range(WIDE):
+        rows = wg[pl.ds(8 * p, 8), :]
+        sums[p] = jnp.concatenate(
+            [rows[:, :TILE], rows[:, TILE:]], axis=0
+        ).astype(BF)
+    remote = WIDE // QUADS
+    for i in range(remote):
+        at = pl.ds(i * QUADS, QUADS)
+        bound[at] = gbt[i].T.astype(BF).reshape(QUADS, SLOT, TILE)
+        total = gbt[remote + i].T
+        for k in range(NARROW):
+            rows = [total[q * SLOT + k * HUB :][:HUB] for q in range(QUADS)]
+            hub_out[k, pl.ds(i * SLOT, SLOT), :] = jnp.concatenate(rows, axis=0).astype(BF)
     for i in range(DST // blocks):
         out_hidden(i).wait()
 
 
-def forward(list_f, wbuf, buf, cotb, w2, bias):
+def forward(list_f, list_r, cot, wbuf, buf, w2, bias):
     vmem = pl.BlockSpec(memory_space=pltpu.VMEM)
     hbm = pl.BlockSpec(memory_space=pltpu.HBM)
     return pl.pallas_call(
         forward_kernel,
         out_shape=(
             jax.ShapeDtypeStruct((DST * TILE, 2 * TILE), BF),
-            pltpu.VMEM((DST, TILE, TILE), BF),
             pltpu.VMEM((DST * TILE, 2 * TILE), BF),
+            pltpu.VMEM((DST + 1, TILE, TILE), BF),
+            pltpu.VMEM((WIDE, 16, TILE), BF),
+            pltpu.VMEM((WIDE, SLOT, TILE), BF),
+            pltpu.VMEM((NARROW, WIDE * HUB + 16, TILE), BF),
         ),
-        in_specs=[hbm] + [vmem] * 5,
-        out_specs=(hbm, vmem, vmem),
+        in_specs=[hbm] * 3 + [vmem] * 4,
+        out_specs=(hbm,) + (vmem,) * 5,
         scratch_shapes=[
             pltpu.SMEM((4, SLOTS), I32),
+            pltpu.SMEM((4, SLOTS), I32),
+            pltpu.VMEM((DST * TILE, 2 * TILE), BF),
             pltpu.VMEM((DST + 1, TILE, TILE), F32),
             pltpu.VMEM((DST * TILE, 2 * TILE), BF),
-            pltpu.SemaphoreType.DMA((1,)),
+            pltpu.VMEM((SRC - DST + 1, TILE, TILE), F32),
+            pltpu.VMEM((2 * TILE, 2 * TILE), F32),
+            pltpu.VMEM((8, 2 * TILE), F32),
+            pltpu.SemaphoreType.DMA((3,)),
             pltpu.SemaphoreType.DMA((DST * TILE // ROWS,)),
         ],
         compiler_params=pltpu.CompilerParams(vmem_limit_bytes=VMEM_LIMIT),
-    )(in_hbm(list_f), *map(in_vmem, (wbuf, buf, cotb, w2, bias)))
+    )(*map(in_hbm, (list_f, list_r, cot)), *map(in_vmem, (wbuf, buf, w2, bias)))
 
 
 def backward_kernel(
-    lists_b, hub_rows, send_rows, wbuf, buf, w2, aggregate, grad_pre, acc, whole, total_bias,
-    list_b, hub_at, send_at, slots, gt, wg, gb, sums, bound, hubs,
-    back, sum_in, hub_in, sum_out, sum_near, hub_out, hub_near, part,
-    s_back, r_back, s_sum, r_sum, s_hub, r_hub, s_part, r_part,
+    lists_o, hub_rows, send_rows, wbuf, w2, grad_pre, gt, sums, bound, hub_out,
+    acc, whole, total_bias,
+    list_o, hub_at, send_at, slots, back, sum_in, hub_in, sum_out, sum_near, hub_near, hub_part,
+    part, s_back, r_back, s_sum, r_sum, s_hub, r_hub, s_part, r_part,
     s_sum_near, r_sum_near, s_hub_near, r_hub_near, s_in,
 ):
     w = lax.axis_index("wide")
     n = lax.axis_index("narrow")
     loads = [
-        pltpu.make_async_copy(lists_b, list_b, s_in.at[0]),
+        pltpu.make_async_copy(lists_o, list_o, s_in.at[0]),
         pltpu.make_async_copy(hub_rows, hub_at, s_in.at[1]),
         pltpu.make_async_copy(send_rows, send_at, s_in.at[2]),
     ]
     for c in loads:
         c.start()
     barrier = greet_all(w, n)
-    gb[...] = jnp.zeros_like(gb)
-    wg[...] = jnp.zeros_like(wg)
-    gt[DST] = jnp.zeros((TILE, TILE), BF)
     slots[PAIRS] = jnp.zeros((TILE, TILE), F32)
-    blocks = ROWS // TILE
-
-    def dense(i, c):
-        rows = pl.ds(i * ROWS, ROWS)
-        f = buf[pl.ds(i * blocks * QUADS, blocks * QUADS)].reshape(ROWS, TILE)
-        x = jnp.concatenate([f, aggregate[pl.ds(i * blocks, blocks)].reshape(ROWS, TILE)], axis=1)
-        gp = grad_pre[rows, :]
-        wg[...] += tn(x, gp)
-        gb[...] += jnp.sum(gp.astype(F32).reshape(ROWS // 8, 8, 2 * TILE), axis=0)
-        acc[rows, :] = nt(gp, w2[pl.ds(0, TILE), :])
-        g = nt(w2[pl.ds(TILE, TILE), :], gp).astype(BF)
-        for j in range(blocks):
-            gt[i * blocks + j] = g[:, j * TILE : (j + 1) * TILE]
-        return c
-
-    lax.fori_loop(0, DST // blocks, dense, 0)
-    bias_sum = jnp.sum(gb[...], axis=0, keepdims=True)
-    row = iota((16, TILE), 0)
-    bias_rows = jnp.where(
-        row == 0, bias_sum[:, :TILE], jnp.where(row == 1, bias_sum[:, TILE:], 0.0)
-    ).astype(BF)
-    for p in range(WIDE):
-        rows = wg[pl.ds(8 * p, 8), :]
-        sums[p, pl.ds(0, 16), :] = jnp.concatenate(
-            [rows[:, :TILE], rows[:, TILE:]], axis=0
-        ).astype(BF)
-        sums[p, pl.ds(16, 16), :] = bias_rows
+
     pl.semaphore_wait(barrier, WIDE - 1 + NARROW - 1)
 
     def wide_copy(o, src, dst, send, recv):
@@ -436,7 +469,7 @@
         return wide_copy(o, sums.at[lax.rem(w + o, WIDE)], sum_in.at[slot], s_sum, r_sum)
 
     def hub_copy(o, slot):
-        return wide_copy(o, hubs.at[lax.rem(w + o, WIDE)], hub_in.at[slot], s_hub, r_hub)
+        return wide_copy(o, hub_part.at[lax.rem(w + o, WIDE)], hub_in.at[slot], s_hub, r_hub)
 
     def back_copy(o, slot):
         return wide_copy(o, bound.at[lax.rem(w + o, WIDE)], back.at[slot], s_back, r_back)
@@ -473,58 +506,55 @@
         def one(q, total):
             return total + ref[q].astype(F32)
 
-        return lax.fori_loop(0, WIDE, one, jnp.zeros((rows, TILE), F32))
+        return lax.fori_loop(0, WIDE, one, jnp.zeros((rows, TILE), F32), unroll=4)
 
     def walk(i, total):
         parts = []
-        for u in range(UNROLL):
-            k = 2 * (i * UNROLL + u)
-            left = jnp.concatenate([gt[list_b[1, k]], gt[list_b[1, k + 1]]], axis=1)
-            right = jnp.concatenate([wbuf[list_b[0, k]], wbuf[list_b[0, k + 1]]], axis=0)
+        for u in range(WALK):
+            k = 2 * (i * WALK + u)
+            left = jnp.concatenate([gt[list_o[1, k]], gt[list_o[1, k + 1]]], axis=1)
+            right = jnp.concatenate([wbuf[list_o[0, k]], wbuf[list_o[0, k + 1]]], axis=0)
             parts.append(mm(left, right))
-        for u in range(UNROLL):
-            k = i * UNROLL + u
-            same = list_b[2, 2 * k] == list_b[2, jnp.maximum(2 * k - 2, 0)]
+        for u in range(WALK):
+            k = i * WALK + u
+            same = list_o[2, 2 * k] == list_o[2, jnp.maximum(2 * k - 2, 0)]
             total = total * same.astype(F32) + parts[u]
             slots[k] = total
         return total
 
     send(sum_copy)
+    for k in range(1, NARROW):
+        hub_near_copy(k, n).start()
+    send(back_copy)
     sum_in[w] = sums[w]
+    back[w] = bound[w]
+    hub_near[n] = hub_out[n]
     for c in loads:
         c.wait()
-    steps = PAIRS // UNROLL
-    total = lax.fori_loop(0, steps // 2, walk, jnp.zeros((TILE, TILE), F32))
+    def own_part(i, c):
+        rows = pl.ds(i * ROWS, ROWS)
+        acc[rows, :] = nt(grad_pre[rows, :], w2[pl.ds(0, TILE), :])
+        return c
+
+    lax.fori_loop(0, DST * TILE // ROWS, own_part, 0)
+    lax.fori_loop(0, PAIRS // WALK, walk, jnp.zeros((TILE, TILE), F32))
+
     arrive(sum_copy)
-    sum_out[...] = add_up(sum_in, SLOT)[:24]
+    sum_out[...] = add_up(sum_in, 16)
     sum_near[n] = sum_out[...]
     for k in range(1, NARROW):
         sum_near_copy(k, n).start()
-    lax.fori_loop(steps // 2, steps, walk, total)
-    near_arrive(sum_near_copy)
-    near = sum_near[0] + sum_near[1] + sum_near[2] + sum_near[3]
-    part[...] = near[0:16].astype(BF)
-    whole[w] = near[0:16].astype(BF)
-    total_bias[...] = near[16:24]
-
-    remote = WIDE // QUADS
-    for i in range(remote):
-        at = pl.ds(i * QUADS, QUADS)
-        total = slots[list_b[3, DST + remote + i]]
-        hubs[at] = total.T.astype(BF).reshape(QUADS, SLOT, TILE)
+    near_arrive(hub_near_copy)
+    hub_sum = sum(hub_near[k].astype(F32) for k in range(NARROW))
+    hub_part[:, pl.ds(0, HUB), :] = hub_sum[: WIDE * HUB].reshape(WIDE, HUB, TILE)
+    bias_part = hub_sum[WIDE * HUB : WIDE * HUB + HUB]
+    hub_part[:, pl.ds(HUB, HUB), :] = jnp.broadcast_to(bias_part, (WIDE, HUB, TILE))
     send(hub_copy)
-    for i in range(remote):
-        at = pl.ds(i * QUADS, QUADS)
-        total = slots[list_b[3, DST + i]]
-        bound[at] = total.T.astype(BF).reshape(QUADS, SLOT, TILE)
-    send(back_copy)
-    send(part_copy)
-    hub_in[w] = hubs[w]
-    back[w] = bound[w]
+    hub_in[w] = hub_part[w]
 
     def add_own(i, c):
         at = pl.ds(i * TILE, TILE)
-        acc[at, :] += slots[list_b[3, i]].T
+        acc[at, :] += slots[list_o[3, i]].T
         return c
 
     lax.fori_loop(0, DST, add_own, 0, unroll=4)
@@ -533,34 +563,41 @@
     for j in range(HUB):
         hub_lane = jnp.where((lane == j) | (lane == j + HUB), hub_at[j], hub_lane)
     row_lane = jnp.concatenate([send_at[pl.ds(p, 1), :] for p in range(WIDE)], axis=1)
-
+    step = 256
+    base = iota((step, TILE), 0).astype(F32).astype(BF)
+    one, zero = jnp.ones((), BF), jnp.zeros((), BF)
+
+    def scatter(lanes, values, first, last):
+        def add(i, c):
+            at = pl.ds(i * step, step)
+            near_by = jnp.clip(lanes - i * step, -1, step).astype(F32).astype(BF)
+            hot = [
+                jnp.where(base == near_by[:, c : c + TILE], one, zero)
+                for c in range(0, lanes.shape[1], TILE)
+            ]
+            acc[at, :] += mm(jnp.concatenate(hot, axis=1), values)
+            return c
+
+        lax.fori_loop(first, last, add, 0, unroll=4)
+
+    arrive(back_copy)
+    pieces = DST * TILE // step
+    returned = back[...].reshape(WIDE * SLOT, TILE)
+    scatter(row_lane, returned, 0, pieces // 2)
+    near_arrive(sum_near_copy)
+    near = sum_near[0] + sum_near[1] + sum_near[2] + sum_near[3]
+    part[...] = near.astype(BF)
+    whole[w] = near.astype(BF)
+    send(part_copy)
+    scatter(row_lane, returned, pieces // 2, pieces)
     arrive(hub_copy)
-    hub_sum = add_up(hub_in, SLOT)
-    for k in range(NARROW):
-        hub_out[k] = hub_sum[HUB * k : HUB * (k + 1)]
-    hub_near[n] = hub_out[n]
-    for k in range(1, NARROW):
-        hub_near_copy(k, n).start()
-
-    def scatter(lanes, values):
-        step = 512
-
-        def one(i, c):
-            at = pl.ds(i * step, step)
-            hit = iota((step, lanes.shape[1]), 0) + i * step == lanes
-            acc[at, :] += mm(jnp.where(hit, 1.0, 0.0).astype(BF), values)
-            return c
-
-        lax.fori_loop(0, DST * TILE // step, one, 0)
-
-    arrive(back_copy)
-    scatter(row_lane, back[...].reshape(WIDE * SLOT, TILE))
-    near_arrive(hub_near_copy)
-    mine = hub_near[0] + hub_near[1] + hub_near[2] + hub_near[3]
+    got = add_up(hub_in, 2 * HUB)
+    mine = got[:HUB]
+    total_bias[...] = got[HUB:]
     high = mine.astype(BF)
     low = (mine - high.astype(F32)).astype(BF)
     values = jnp.concatenate([high, low, jnp.zeros((TILE - 2 * HUB, TILE), BF)], axis=0)
-    scatter(hub_lane, values)
+    scatter(hub_lane, values, 0, pieces)
     arrive(part_copy)
 
     def sent(o, c):
@@ -576,7 +613,7 @@
         hub_near_copy(k, n).wait_send()
 
 
-def backward(list_b, hub_rows, send_rows, wbuf, buf, w2, aggregate, grad_pre):
+def backward(list_o, hub_rows, send_rows, wbuf, w2, grad_pre, gt, sums, bound, hub_out):
     vmem = pl.BlockSpec(memory_space=pltpu.VMEM)
     hbm = pl.BlockSpec(memory_space=pltpu.HBM)
     dma = pltpu.SemaphoreType.DMA
@@ -587,26 +624,20 @@
             pltpu.VMEM((WIDE, 16, TILE), BF),
             pltpu.VMEM((8, TILE), F32),
         ),
-        in_specs=[hbm] * 3 + [vmem] * 5,
+        in_specs=[hbm] * 3 + [vmem] * 7,
         out_specs=(vmem,) * 3,
         scratch_shapes=[
             pltpu.SMEM((4, SLOTS), I32),
             pltpu.SMEM((HUB,), I32),
             pltpu.VMEM((WIDE, SLOT), I32),
             pltpu.VMEM((PAIRS + 1, TILE, TILE), F32),
-            pltpu.VMEM((DST + 1, TILE, TILE), BF),
-            pltpu.VMEM((2 * TILE, 2 * TILE), F32),
-            pltpu.VMEM((8, 2 * TILE), F32),
             pltpu.VMEM((WIDE, SLOT, TILE), BF),
-            pltpu.VMEM((WIDE, SLOT, TILE), BF),
-            pltpu.VMEM((WIDE, SLOT, TILE), BF),
-            pltpu.VMEM((WIDE, SLOT, TILE), BF),
-            pltpu.VMEM((WIDE, SLOT, TILE), BF),
-            pltpu.VMEM((WIDE, SLOT, TILE), BF),
-            pltpu.VMEM((24, TILE), F32),
-            pltpu.VMEM((NARROW, 24, TILE), F32),
-            pltpu.VMEM((NARROW, HUB, TILE), F32),
-            pltpu.VMEM((NARROW, HUB, TILE), F32),
+            pltpu.VMEM((WIDE, 16, TILE), BF),
+            pltpu.VMEM((WIDE, 2 * HUB, TILE), F32),
+            pltpu.VMEM((16, TILE), F32),
+            pltpu.VMEM((NARROW, 16, TILE), F32),
+            pltpu.VMEM((NARROW, WIDE * HUB + 16, TILE), BF),
+            pltpu.VMEM((WIDE, 2 * HUB, TILE), F32),
             pltpu.VMEM((16, TILE), BF),
             dma((WIDE,)), dma((WIDE,)), dma((WIDE,)), dma((WIDE,)),
             dma((WIDE,)), dma((WIDE,)), dma((WIDE,)), dma((WIDE,)),
@@ -616,8 +647,8 @@
             collective_id=1, has_side_effects=True, vmem_limit_bytes=VMEM_LIMIT
         ),
     )(
-        in_hbm(list_b), in_hbm(hub_rows), in_hbm(send_rows),
-        *map(in_vmem, (wbuf, buf, w2, aggregate, grad_pre)),
+        *map(in_hbm, (list_o, hub_rows, send_rows)),
+        *map(in_vmem, (wbuf, w2, grad_pre, gt, sums, bound, hub_out)),
     )
 
 
@@ -665,15 +696,17 @@
     send_rows, hub_rows,
 ):
     lanes = (TILES // TILE, TILE)
-    wbuf, buf, cotb, w2, b2, list_f, list_b = fetch(
-        features.reshape(DST * QUADS, SLOT, TILE), cotangent, w_self, w_neigh,
+    wbuf, buf, w2, b2, list_f, list_r, list_o = fetch(
+        features.reshape(DST * QUADS, SLOT, TILE), w_self, w_neigh,
         bias.reshape(1, 2 * TILE), tile_weights,
         tile_src.reshape(lanes), tile_dst.reshape(lanes), tile_live.reshape(lanes),
         send_rows, hub_rows,
     )
-    hidden, aggregate, grad_pre = forward(list_f, wbuf, buf, cotb, w2, b2)
+    hidden, grad_pre, gt, sums, bound, hub_out = forward(
+        list_f, list_r, cotangent, wbuf, buf, w2, b2
+    )
     acc, whole, total_bias = backward(
-        list_b, hub_rows, send_rows, wbuf, buf, w2, aggregate, grad_pre
+        list_o, hub_rows, send_rows, wbuf, w2, grad_pre, gt, sums, bound, hub_out
     )
     grad_features, grad_self, grad_neigh, grad_bias = finish(acc, whole, total_bias)
     return (hidden, grad_features, grad_self, grad_neigh, grad_bias.reshape(2 * TILE))

time: 65 us -> 59.7 us (0.918)
  Pallas kernels: 64.1 us -> 58.4 us
    pallas_call x1, Pallas kernels: 32.3 us -> 24.1 us  [backward(): pl.pallas_call(backward_kernel, out_shape=(pltpu.VMEM((DST * TILE, TILE),...]
    pallas_call x1, Pallas kernels: 10.9 us -> 13.4 us  [forward(): pl.pallas_call(forward_kernel, out_shape=(jax.ShapeDtypeStruct((DST * TIL...]
where the time goes in v4:
time: 59.7 us; the launch traced here: 59 us
  Pallas kernels  58.4 us (98%)
  between operations  0.66 us (1%)
    pallas_call x1, Pallas kernels, backward(): pl.pallas_call(backward_kernel, out_shape=(pltpu.VMEM((DST * TILE, TILE),...  24.1 us
    pallas_call x1, Pallas kernels, fetch(): pl.pallas_call(fetch_kernel, out_shape=(pltpu.VMEM((TILES, TILE, TILE), B...  19.4 us
    pallas_call x1, Pallas kernels, forward(): pl.pallas_call(forward_kernel, out_shape=(jax.ShapeDtypeStruct((DST * TIL...  13.4 us
    pallas_call x1, Pallas kernels, finish(): pl.pallas_call(finish_kernel, out_shape=(jax.ShapeDtypeStruct((DST * TILE...  1.43 us

profile of v4, /device:TPU:1, one launch (start us, length us, event | category | flops | bytes accessed | tf_op | source)
XLA Modules:
  0.0 59.0 jit_solution(646974142669584698)
XLA Ops:
  0.6 19.4 %shard_map.146 = (bf16[512,128,128]{2,1,0:T(8,128)(2,1)S(1)}, bf16[196,32,128]{2,1,0:T(8,128)(2,1)S(1)}, bf16[256,256]{1,0:T(8,128)(2,1)S(1)}, f32[1,256]{1,0:T(...) custom-call(bf16[128,32,128]{2,1,0:T(8,128)(2,1)} %bitcast.6, bf16[128,256]{1,0:T(8,128)(2,1)} %w_self.1, ...), custom_call_target="tpu_custom_call" | custom-call | tf_op jit(solution)/shard_map/pallas_call | solution.py:252
  20.0 13.4 %shard_map.147 = (bf16[4096,256]{1,0:T(8,128)(2,1)}, bf16[4096,256]{1,0:T(8,128)(2,1)S(1)}, bf16[33,128,128]{2,1,0:T(8,128)(2,1)S(1)}, bf16[32,16,128]{2,1,0:T(8...) custom-call(s32[4,640]{1,0:T(4,128)} %get-tuple-element.25.lists_f, ...), custom_call_target="tpu_custom_call" | custom-call | tf_op jit(solution)/shard_map/pallas_call | solution.py:399
  33.5 24.1 %shard_map.148 = (f32[4096,128]{1,0:T(8,128)S(1)}, bf16[32,16,128]{2,1,0:T(8,128)(2,1)S(1)}, f32[8,128]{1,0:T(8,128)S(1)}) custom-call(s32[4,640]{1,0:T(4,128)} %get-tuple-element.32.lists_o, s32[8]{0:T(128)} %hub_rows.3, s32[32,32]{1,0:T(8,128)} %send_rows.3, bf16[512,128,128]{2,1,0:T(8,128)(2,1)S(1)} %get-tuple-element.27.wbuf, ...), custom_call_target="tpu_custom_call" | custom-call | tf_op jit(solution)/shard_map/pallas_call | solution.py:620
  57.6 1.4 %shard_map.149 = (f32[4096,128]{1,0:T(8,128)}, f32[128,256]{1,0:T(8,128)}, f32[128,256]{1,0:T(8,128)}, f32[1,256]{1,0:T(1,128)}) custom-call(f32[4096,128]{1,0:T(8,128)S(1)} %get-tuple-element.38.acc, bf16[32,16,128]{2,1,0:T(8,128)(2,1)S(1)} %get-tuple-element.39.whole, f32[8,128]{1,0:T(8,128)S(1)} %get-tuple-element.40.total_bias), custom_call_target="tpu_custom_call" | custom-call | tf_op jit(solution)/shard_map/pallas_call | solution.py:676

commit v5 on v4

--- a/solution.py
+++ b/solution.py
@@ -18,8 +18,9 @@
 WALK = 34
 PAIRS = 272
 COUNT = 64
-ROWS = 1024
+ROWS = 4096
 CHUNKS = 8
+FIRST = 6
 VMEM_LIMIT = 32 * 2**20
 SLOT = 32
 QUADS = TILE // SLOT
@@ -537,33 +538,18 @@
         return c
 
     lax.fori_loop(0, DST * TILE // ROWS, own_part, 0)
-    lax.fori_loop(0, PAIRS // WALK, walk, jnp.zeros((TILE, TILE), F32))
-
-    arrive(sum_copy)
-    sum_out[...] = add_up(sum_in, 16)
-    sum_near[n] = sum_out[...]
-    for k in range(1, NARROW):
-        sum_near_copy(k, n).start()
-    near_arrive(hub_near_copy)
-    hub_sum = sum(hub_near[k].astype(F32) for k in range(NARROW))
-    hub_part[:, pl.ds(0, HUB), :] = hub_sum[: WIDE * HUB].reshape(WIDE, HUB, TILE)
-    bias_part = hub_sum[WIDE * HUB : WIDE * HUB + HUB]
-    hub_part[:, pl.ds(HUB, HUB), :] = jnp.broadcast_to(bias_part, (WIDE, HUB, TILE))
-    send(hub_copy)
-    hub_in[w] = hub_part[w]
-
     def add_own(i, c):
         at = pl.ds(i * TILE, TILE)
         acc[at, :] += slots[list_o[3, i]].T
         return c
 
-    lax.fori_loop(0, DST, add_own, 0, unroll=4)
     lane = iota((1, TILE), 1)
     hub_lane = jnp.full((1, TILE), -1, I32)
     for j in range(HUB):
         hub_lane = jnp.where((lane == j) | (lane == j + HUB), hub_at[j], hub_lane)
     row_lane = jnp.concatenate([send_at[pl.ds(p, 1), :] for p in range(WIDE)], axis=1)
     step = 256
+    pieces = DST * TILE // step
     base = iota((step, TILE), 0).astype(F32).astype(BF)
     one, zero = jnp.ones((), BF), jnp.zeros((), BF)
 
@@ -580,16 +566,47 @@
 
         lax.fori_loop(first, last, add, 0, unroll=4)
 
+    def walk_on(first, last, total):
+        return lax.fori_loop(first, last, walk, total)
+
+    def own_sums():
+        lax.fori_loop(0, DST, add_own, 0, unroll=4)
+
+    def sums_arrived():
+        arrive(sum_copy)
+        sum_out[...] = add_up(sum_in, 16)
+        sum_near[n] = sum_out[...]
+        for k in range(1, NARROW):
+            sum_near_copy(k, n).start()
+
+    def hubs_near_by():
+        near_arrive(hub_near_copy)
+        hub_sum = sum(hub_near[k].astype(F32) for k in range(NARROW))
+        hub_part[:, pl.ds(0, HUB), :] = hub_sum[: WIDE * HUB].reshape(WIDE, HUB, TILE)
+        bias_part = hub_sum[WIDE * HUB : WIDE * HUB + HUB]
+        hub_part[:, pl.ds(HUB, HUB), :] = jnp.broadcast_to(bias_part, (WIDE, HUB, TILE))
+        send(hub_copy)
+        hub_in[w] = hub_part[w]
+
+    def sums_near_by():
+        near_arrive(sum_near_copy)
+        near = sum_near[0] + sum_near[1] + sum_near[2] + sum_near[3]
+        part[...] = near.astype(BF)
+        whole[w] = near.astype(BF)
+        send(part_copy)
+
+    def rows_back(first, last):
+        scatter(row_lane, back[...].reshape(WIDE * SLOT, TILE), first, last)
+
+    steps = PAIRS // WALK
+    total = walk_on(0, FIRST, jnp.zeros((TILE, TILE), F32))
+    sums_arrived()
+    walk_on(FIRST, steps, total)
+    hubs_near_by()
+    own_sums()
+    sums_near_by()
     arrive(back_copy)
-    pieces = DST * TILE // step
-    returned = back[...].reshape(WIDE * SLOT, TILE)
-    scatter(row_lane, returned, 0, pieces // 2)
-    near_arrive(sum_near_copy)
-    near = sum_near[0] + sum_near[1] + sum_near[2] + sum_near[3]
-    part[...] = near.astype(BF)
-    whole[w] = near.astype(BF)
-    send(part_copy)
-    scatter(row_lane, returned, pieces // 2, pieces)
+    rows_back(0, pieces)
     arrive(hub_copy)
     got = add_up(hub_in, 2 * HUB)
     mine = got[:HUB]

time: 59.7 us -> 57.3 us (0.960)
  Pallas kernels: 58.4 us -> 55.8 us
    pallas_call x1, Pallas kernels: 24.1 us -> 22.5 us  [backward(): pl.pallas_call(backward_kernel, out_shape=(pltpu.VMEM((DST * TILE, TILE),...]
    pallas_call x1, Pallas kernels: 13.4 us -> 12.5 us  [forward(): pl.pallas_call(forward_kernel, out_shape=(jax.ShapeDtypeStruct((DST * TIL...]
where the time goes in v5:
time: 57.3 us; the launch traced here: 56.4 us
  Pallas kernels  55.8 us (97%)
  between operations  0.66 us (1%)
    pallas_call x1, Pallas kernels, backward(): pl.pallas_call(backward_kernel, out_shape=(pltpu.VMEM((DST * TILE, TILE),...  22.5 us
    pallas_call x1, Pallas kernels, fetch(): pl.pallas_call(fetch_kernel, out_shape=(pltpu.VMEM((TILES, TILE, TILE), B...  19.4 us
    pallas_call x1, Pallas kernels, forward(): pl.pallas_call(forward_kernel, out_shape=(jax.ShapeDtypeStruct((DST * TIL...  12.5 us
    pallas_call x1, Pallas kernels, finish(): pl.pallas_call(finish_kernel, out_shape=(jax.ShapeDtypeStruct((DST * TILE...  1.43 us

profile of v5, /device:TPU:1, one launch (start us, length us, event | category | flops | bytes accessed | tf_op | source)
XLA Modules:
  0.0 56.4 jit_solution(4161134867143483377)
XLA Ops:
  0.6 19.4 %shard_map.146 = (bf16[512,128,128]{2,1,0:T(8,128)(2,1)S(1)}, bf16[196,32,128]{2,1,0:T(8,128)(2,1)S(1)}, bf16[256,256]{1,0:T(8,128)(2,1)S(1)}, f32[1,256]{1,0:T(...) custom-call(bf16[128,32,128]{2,1,0:T(8,128)(2,1)} %bitcast.6, bf16[128,256]{1,0:T(8,128)(2,1)} %w_self.1, ...), custom_call_target="tpu_custom_call" | custom-call | tf_op jit(solution)/shard_map/pallas_call | solution.py:253
  20.0 12.5 %shard_map.147 = (bf16[4096,256]{1,0:T(8,128)(2,1)}, bf16[4096,256]{1,0:T(8,128)(2,1)S(1)}, bf16[33,128,128]{2,1,0:T(8,128)(2,1)S(1)}, bf16[32,16,128]{2,1,0:T(8...) custom-call(s32[4,640]{1,0:T(4,128)} %get-tuple-element.25.lists_f, ...), custom_call_target="tpu_custom_call" | custom-call | tf_op jit(solution)/shard_map/pallas_call | solution.py:400
  32.5 22.5 %shard_map.148 = (f32[4096,128]{1,0:T(8,128)S(1)}, bf16[32,16,128]{2,1,0:T(8,128)(2,1)S(1)}, f32[8,128]{1,0:T(8,128)S(1)}) custom-call(s32[4,640]{1,0:T(4,128)} %get-tuple-element.32.lists_o, s32[8]{0:T(128)} %hub_rows.3, s32[32,32]{1,0:T(8,128)} %send_rows.3, bf16[512,128,128]{2,1,0:T(8,128)(2,1)S(1)} %get-tuple-element.27.wbuf, ...), custom_call_target="tpu_custom_call" | custom-call | tf_op jit(solution)/shard_map/pallas_call | solution.py:637
  55.0 1.4 %shard_map.149 = (f32[4096,128]{1,0:T(8,128)}, f32[128,256]{1,0:T(8,128)}, f32[128,256]{1,0:T(8,128)}, f32[1,256]{1,0:T(1,128)}) custom-call(f32[4096,128]{1,0:T(8,128)S(1)} %get-tuple-element.38.acc, bf16[32,16,128]{2,1,0:T(8,128)(2,1)S(1)} %get-tuple-element.39.whole, f32[8,128]{1,0:T(8,128)S(1)} %get-tuple-element.40.total_bias), custom_call_target="tpu_custom_call" | custom-call | tf_op jit(solution)/shard_map/pallas_call | solution.py:693

commit v6 on v5

--- a/solution.py
+++ b/solution.py
@@ -20,7 +20,7 @@
 COUNT = 64
 ROWS = 4096
 CHUNKS = 8
-FIRST = 6
+FIRST = 7
 VMEM_LIMIT = 32 * 2**20
 SLOT = 32
 QUADS = TILE // SLOT
@@ -300,6 +300,14 @@
         return c
 
     lax.fori_loop(0, DST + 1, clear, 0)
+    def clear_back(i, c):
+        gbt[i] = jnp.zeros((TILE, TILE), F32)
+        return c
+
+    lax.fori_loop(0, SRC - DST + 1, clear_back, 0)
+    gb[...] = jnp.zeros_like(gb)
+    wg[...] = jnp.zeros_like(wg)
+    gt[DST] = jnp.zeros((TILE, TILE), BF)
     loads[0].wait()
 
     def rows_of(s):
@@ -319,14 +327,6 @@
         return c
 
     lax.fori_loop(0, (list_f[3, COUNT] + UNROLL - 1) // UNROLL, step, 0)
-    def clear_back(i, c):
-        gbt[i] = jnp.zeros((TILE, TILE), F32)
-        return c
-
-    lax.fori_loop(0, SRC - DST + 1, clear_back, 0)
-    gb[...] = jnp.zeros_like(gb)
-    wg[...] = jnp.zeros_like(wg)
-    gt[DST] = jnp.zeros((TILE, TILE), BF)
     for c in loads[1:]:
         c.wait()
     blocks = ROWS // TILE

time: 57.3 us -> 57.4 us (level); the launches traced: 56.4 us -> 57.1 us
  Pallas kernels: 55.8 us -> 56.5 us
    pallas_call x1, Pallas kernels: 22.5 us -> 23.3 us  [backward(): pl.pallas_call(backward_kernel, out_shape=(pltpu.VMEM((DST * TILE, TILE),...]
where the time goes in v6:
time: 57.4 us; the launch traced here: 57.1 us
  Pallas kernels  56.5 us (98%)
  between operations  0.66 us (1%)
    pallas_call x1, Pallas kernels, backward(): pl.pallas_call(backward_kernel, out_shape=(pltpu.VMEM((DST * TILE, TILE),...  23.3 us
    pallas_call x1, Pallas kernels, fetch(): pl.pallas_call(fetch_kernel, out_shape=(pltpu.VMEM((TILES, TILE, TILE), B...  19.4 us
    pallas_call x1, Pallas kernels, forward(): pl.pallas_call(forward_kernel, out_shape=(jax.ShapeDtypeStruct((DST * TIL...  12.4 us
    pallas_call x1, Pallas kernels, finish(): pl.pallas_call(finish_kernel, out_shape=(jax.ShapeDtypeStruct((DST * TILE...  1.43 us

profile of v6, /device:TPU:1, one launch (start us, length us, event | category | flops | bytes accessed | tf_op | source)
XLA Modules:
  0.0 57.1 jit_solution(7953157988151388384)
XLA Ops:
  0.6 19.4 %shard_map.146 = (bf16[512,128,128]{2,1,0:T(8,128)(2,1)S(1)}, bf16[196,32,128]{2,1,0:T(8,128)(2,1)S(1)}, bf16[256,256]{1,0:T(8,128)(2,1)S(1)}, f32[1,256]{1,0:T(...) custom-call(bf16[128,32,128]{2,1,0:T(8,128)(2,1)} %bitcast.6, bf16[128,256]{1,0:T(8,128)(2,1)} %w_self.1, ...), custom_call_target="tpu_custom_call" | custom-call | tf_op jit(solution)/shard_map/pallas_call | solution.py:253
  20.0 12.4 %shard_map.147 = (bf16[4096,256]{1,0:T(8,128)(2,1)}, bf16[4096,256]{1,0:T(8,128)(2,1)S(1)}, bf16[33,128,128]{2,1,0:T(8,128)(2,1)S(1)}, bf16[32,16,128]{2,1,0:T(8...) custom-call(s32[4,640]{1,0:T(4,128)} %get-tuple-element.25.lists_f, ...), custom_call_target="tpu_custom_call" | custom-call | tf_op jit(solution)/shard_map/pallas_call | solution.py:400
  32.4 23.3 %shard_map.148 = (f32[4096,128]{1,0:T(8,128)S(1)}, bf16[32,16,128]{2,1,0:T(8,128)(2,1)S(1)}, f32[8,128]{1,0:T(8,128)S(1)}) custom-call(s32[4,640]{1,0:T(4,128)} %get-tuple-element.32.lists_o, s32[8]{0:T(128)} %hub_rows.3, s32[32,32]{1,0:T(8,128)} %send_rows.3, bf16[512,128,128]{2,1,0:T(8,128)(2,1)S(1)} %get-tuple-element.27.wbuf, ...), custom_call_target="tpu_custom_call" | custom-call | tf_op jit(solution)/shard_map/pallas_call | solution.py:637
  55.7 1.4 %shard_map.149 = (f32[4096,128]{1,0:T(8,128)}, f32[128,256]{1,0:T(8,128)}, f32[128,256]{1,0:T(8,128)}, f32[1,256]{1,0:T(1,128)}) custom-call(f32[4096,128]{1,0:T(8,128)S(1)} %get-tuple-element.38.acc, bf16[32,16,128]{2,1,0:T(8,128)(2,1)S(1)} %get-tuple-element.39.whole, f32[8,128]{1,0:T(8,128)S(1)} %get-tuple-element.40.total_bias), custom_call_target="tpu_custom_call" | custom-call | tf_op jit(solution)/shard_map/pallas_call | solution.py:693
